TPU v7x, 768 devices: a whole 4x8x12 slice. The times are simulated.
768 devices in a mesh: dp: 16 (over x, y_hi, core), mp: 48 (over y_lo, z).
Axes of the slice: x: 4, y: 8 (y_hi: 2, y_lo: 4; y = y_hi * 4 + y_lo), z: 12, core: 2. Of those that a mesh axis runs over, the one named last changes fastest.
Arguments:
- tokens: bfloat16 [4096, 6144], P('dp', 'mp'), may hold values from -700 to 700
- ln_gain: float32 [6144], replicated, may hold values from 0.1 to 1.9
- w_qkv: bfloat16 [6144, 18432], P(None, 'mp'), may hold values from -1 to 1
- q_gain: float32 [48, 128], P('mp'), may hold values from 0.4 to 7
- k_gain: float32 [48, 128], P('mp'), may hold values from 0.4 to 7
- d_attn: bfloat16 [4096, 6144], P('dp', 'mp'), may hold values from -0.29882812 to 0.29882812
Outputs:
- grad_qkv: bfloat16 [6144, 18432], P('dp', 'mp')
All inputs are finite; a program needn't handle non-finite values.
Results may differ from a plain program's by a relative error of at most 0.02.
The roundings to bfloat16 on the way count: a program that leaves them out, or rounds other values in their place, can miss the bound.
Values may be sent and summed in bfloat16 or wider, within the bound.
A program may use at most 32 MiB of HBM per device.

v0:
```python
import math

import jax
import jax.numpy as jnp
from jax import lax
from jax.sharding import PartitionSpec as P

SEQ = 256


def norm_rows(activations, gain_row):
    widened = activations.astype(jnp.float32)
    center = jnp.mean(widened, axis=-1, keepdims=True)
    spread = jnp.mean(jnp.square(widened - center), axis=-1, keepdims=True)
    return (widened - center) * lax.rsqrt(spread + 1e-06) * gain_row


def head_norm(vectors):
    center = jnp.mean(vectors, axis=-1, keepdims=True)
    spread = jnp.mean(jnp.square(vectors - center), axis=-1, keepdims=True)
    inverse = lax.rsqrt(spread + 1e-06)
    return ((vectors - center) * inverse, inverse)


def head_norm_back(grad_out, normal, inverse, gain_row):
    scaled = grad_out * gain_row
    first = jnp.mean(scaled, axis=-1, keepdims=True)
    second = jnp.mean(scaled * normal, axis=-1, keepdims=True)
    return inverse * (scaled - first - normal * second)


def contract(normed, gradient):
    return jnp.einsum("rd,rc->dc", normed, gradient, preferred_element_type=jnp.float32)


def local(tokens, ln_gain, w_qkv, q_gain, k_gain, d_attn):
    gathered = lax.all_gather(tokens, "mp", axis=1, tiled=True)
    normed = norm_rows(gathered, ln_gain).astype(jnp.bfloat16)
    head_count = q_gain.shape[0]
    head_width = q_gain.shape[1]
    row_count = gathered.shape[0]
    images = row_count // SEQ
    projected = jnp.dot(normed, w_qkv, preferred_element_type=jnp.float32)
    projected = projected.reshape(images, SEQ, head_count, 3, head_width)
    query_hat, query_inv = head_norm(projected[:, :, :, 0])
    key_hat, key_inv = head_norm(projected[:, :, :, 1])
    query_n = (query_hat * q_gain).astype(jnp.bfloat16)
    key_n = (key_hat * k_gain).astype(jnp.bfloat16)
    values = projected[:, :, :, 2].astype(jnp.bfloat16)
    score_scale = 1.0 / math.sqrt(head_width)
    scores = (
        jnp.einsum("bihd,bjhd->bhij", query_n, key_n, preferred_element_type=jnp.float32)
        * score_scale
    )
    probs = jax.nn.softmax(scores, axis=-1)
    probs_low = probs.astype(jnp.bfloat16)
    upstream = d_attn.reshape(images, SEQ, head_count, head_width)
    grad_value = jnp.einsum(
        "bhij,bihd->bjhd", probs_low, upstream, preferred_element_type=jnp.float32
    )
    grad_prob = jnp.einsum("bihd,bjhd->bhij", upstream, values, preferred_element_type=jnp.float32)
    grad_score = probs * (grad_prob - jnp.sum(probs * grad_prob, axis=-1, keepdims=True))
    grad_score = (grad_score * score_scale).astype(jnp.bfloat16)
    grad_qn = jnp.einsum("bhij,bjhd->bihd", grad_score, key_n, preferred_element_type=jnp.float32)
    grad_kn = jnp.einsum("bhij,bihd->bjhd", grad_score, query_n, preferred_element_type=jnp.float32)
    grad_query = head_norm_back(grad_qn, query_hat, query_inv, q_gain)
    grad_key = head_norm_back(grad_kn, key_hat, key_inv, k_gain)
    joined = jnp.stack([grad_query, grad_key, grad_value], axis=3)
    joined = joined.reshape(row_count, head_count * 3 * head_width).astype(jnp.bfloat16)
    summed = lax.psum_scatter(
        contract(normed, joined).astype(jnp.bfloat16), "dp", scatter_dimension=0, tiled=True
    )
    return summed


def solution(mesh):
    placed = (P("dp", "mp"), P(), P(None, "mp"), P("mp", None), P("mp", None), P("dp", "mp"))
    return jax.shard_map(
        local, mesh=mesh, in_specs=placed, out_specs=P("dp", "mp"), check_vma=False
    )
```

profile of v0, /device:TPU:1, one launch (start us, length us, event | category | flops | bytes accessed | tf_op | source)
XLA Modules:
  0.0 350.0 jit_solution(17957701732656107504)
XLA Ops:
  6.5 0.7 all-gather.2.cloned.1.call-update
  7.3 0.0 reduce-scatter.2.cloned.1.call-start
  7.3 174.1 %all-gather.2.cloned.1.call-done = bf16[256,6144]{1,0:T(8,128)(2,1)} async-done(((bf16[256,128]{1,0:T(8,128)(2,1)}), bf16[256,6144]{1,0:T(8,128)(2,1)}) %all-gather.2.cloned.1.call-update) | async-done | bytes 3145744 | tf_op jit(solution)/shard_map/all_gather | solution.py:37
  181.4 2.5 convert_reduce_fusion
  183.9 0.3 copy-done.1
  184.2 1.0 fusion.2
  185.2 0.0 copy-start.5
  185.2 4.6 %fusion.57 = f32[256,384]{0,1:T(8,128)S(1)} fusion(bf16[6144,384]{1,0:T(8,128)(2,1)} %param.8, bf16[256,6144]{1,0:T(8,128)(2,1)S(1)} %copy-done.1, f32[6144]{0:T(1024)S(1)} %copy-done.7, f32[256]{0:T(256)S(1)} %add_rsqrt_fusion.2, f32[256]{0:T(256)S(1)} %broadcast_multiply_fusion.6), kind=kOutput, calls=%fused_computation.87 | convolution fusion | flops 1215823872 | bytes 8284160 | tf_op jit(solution)/shard_map/dot_general | solution.py:43
  190.0 0.3 fusion.59
  190.4 0.1 fusion.9
  190.4 0.2 fusion.7
  190.7 0.2 multiply_reduce_fusion
  190.9 0.1 multiply_convert_fusion
  191.0 0.2 fusion.60
  191.3 0.5 broadcast_multiply_fusion.1
  191.8 0.2 fusion.20
  192.0 0.6 broadcast_multiply_fusion.2
  192.6 0.6 broadcast_multiply_fusion
  193.2 0.6 reduce_sum.116
  193.8 0.7 broadcast_multiply_fusion.3
  194.5 1.0 fusion.38
  195.6 4.9 %convolution_convert_fusion = bf16[6144,384]{1,0:T(8,128)(2,1)} fusion(bf16[256,384]{0,1:T(8,128)(2,1)S(1)} %bitcast.153, bf16[256,6144]{1,0:T(8,128)(2,1)S(1)} %copy-done.1, f32[6144]{0:T(1024)} %param.7, f32[256]{0:T(256)} %copy-done.6, f32[256]{0:T(256)} %copy-done.3), kind=kOutput, calls=%fused_computation | convolution fusion | flops 1218183168 | bytes 8087552 | tf_op jit(solution)/shard_map/rd,rc->dc/dot_general | solution.py:33
  200.4 0.0 reduce-scatter.2.cloned.1.call-update
  200.4 142.7 %reduce-scatter.2.cloned.1.call-done = bf16[384,384]{1,0:T(8,128)(2,1)} async-done(((bf16[6144,384]{1,0:T(8,128)(2,1)}), bf16[384,384]{1,0:T(8,128)(2,1)}) %reduce-scatter.2.cloned.1.call-update) | async-done | bytes 294928 | tf_op jit(solution)/shard_map/reduce_scatter | solution.py:70
  (23 shorter events, 0.2 us)
Async XLA Ops:
  6.5 183.9 %copy-start = (bf16[256,128]{1,0:T(8,128)(2,1)S(1)}, bf16[256,128]{1,0:T(8,128)(2,1)}, u32[]{:S(2)}) copy-start(bf16[256,128]{1,0:T(8,128)(2,1)} %param.11) | copy-start | bytes 196612
  6.5 178.7 %copy-start.7 = (f32[6144]{0:T(1024)S(1)}, f32[6144]{0:T(1024)}, u32[]{:S(2)}) copy-start(f32[6144]{0:T(1024)} %param.7) | copy-start | bytes 73732
  6.5 174.8 %all-gather.2.cloned.1.call-start = ((), (), s32[]{:S(2)}) async-start(), calls=%async_computation.1 | async-start | bytes 3211264 | tf_op jit(solution)/shard_map/all_gather | solution.py:37
  7.3 335.9 %reduce-scatter.2.cloned.1.call-start = ((), (), s32[]{:S(2)}) async-start(), calls=%async_computation.2 | async-start | bytes 5013504 | tf_op jit(solution)/shard_map/reduce_scatter | solution.py:70
  181.4 2.8 copy-start.1
  184.2 5.6 %copy-start.3 = (f32[256]{0:T(256)}, f32[256]{0:T(256)S(1)}, u32[]{:S(2)}) copy-start(f32[256]{0:T(256)S(1)} %broadcast_multiply_fusion.6) | copy-start | bytes 3076
  185.2 4.7 %copy-start.6 = (f32[256]{0:T(256)}, f32[256]{0:T(256)S(1)}, u32[]{:S(2)}) copy-start(f32[256]{0:T(256)S(1)} %add_rsqrt_fusion.2) | copy-start | bytes 3076
  185.2 4.8 %copy-start.4 = (f32[1,128]{1,0:T(1,128)S(1)}, f32[1,128]{1,0:T(1,128)}, u32[]{:S(2)}) copy-start(f32[1,128]{1,0:T(1,128)} %param.10) | copy-start | bytes 1540
  185.2 4.8 %copy-start.5 = (f32[1,128]{1,0:T(1,128)S(1)}, f32[1,128]{1,0:T(1,128)}, u32[]{:S(2)}) copy-start(f32[1,128]{1,0:T(1,128)} %param.9) | copy-start | bytes 1540
  189.9 1.9 copy-start.2
Sparse Core Ops, SparseCore 0:
  9.7 171.6 all-gather.1
  200.6 142.5 reduce-scatter.1
where the time goes:
time: 350 us
  waiting for transfers between devices  318 us (91%)
  between operations  13.5 us (4%)
  matrix products  10.7 us (3%)
  other arithmetic  7.85 us (2%)
    all_gather x1, waiting for transfers between devices, local(): gathered = lax.all_gather(tokens, 'mp', axis=1, tiled=True)  174 us
    reduce_scatter x1, waiting for transfers between devices, local(): lax.psum_scatter(contract(normed, joined).astype(jnp.bfloat16), 'dp', sca...  143 us
  transfers between devices with their start and end apart: 2, of which 2 were waited for; matrix products, arithmetic and copies ran while one was open for 0% of the time, Pallas kernels for 0%

commit v1 on v0

v1 whole, which is shorter than its diff:
```python
import functools
import math

import jax
import jax.numpy as jnp
from jax import lax
from jax.experimental import pallas as pl
from jax.experimental.pallas import tpu as pltpu
from jax.sharding import PartitionSpec as P

MESH = pl.DeviceIdType.MESH
F32 = jnp.float32
BF16 = jnp.bfloat16
SEQ = 256
HD = 128
NX = 4
NYL = 4
NZ = 12
BLOCKS = NYL * NZ
WIDTH = BLOCKS * HD
COLS = 3 * HD
GROUPS = WIDTH // COLS
FAR = NZ // 2
RA = 192
HA = RA // 2
HB = (SEQ - RA) // 2
HALF = COLS // 2


def rdma(src, dst, send, recv, device):
    return pltpu.make_async_remote_copy(
        src_ref=src, dst_ref=dst, send_sem=send, recv_sem=recv, device_id=device, device_id_type=MESH
    )


def head_norm(t):
    center = jnp.mean(t, axis=0, keepdims=True)
    moved = t - center
    spread = jnp.mean(moved * moved, axis=0, keepdims=True)
    inverse = lax.rsqrt(spread + 1e-06)
    return moved * inverse, inverse


def head_norm_back(grad, normal, inverse, gain):
    scaled = grad * gain
    first = jnp.mean(scaled, axis=0, keepdims=True)
    second = jnp.mean(scaled * normal, axis=0, keepdims=True)
    return inverse * (scaled - first - normal * second)


def nt(a, b):
    return lax.dot_general(a, b, (((1,), (1,)), ((), ())), preferred_element_type=F32)


def nn(a, b):
    return jnp.dot(a, b, preferred_element_type=F32)


def body(
    tok, gain, w_hbm, q_gain, k_gain, d_attn, out,
    got, normed, other, w, shift, total, square, proj, joined, joined_other,
    own, part, sx, rx, sy, ry, w_sem,
    s_za, r_za, s_ya, r_ya, s_zb, r_zb, s_yb, r_yb, s_n, r_n, s_j, r_j, s_x, r_x, s_y, r_y,
):
    d = lax.axis_index("dp")
    m = lax.axis_index("mp")
    core = lax.rem(d, 2)
    yh = lax.rem(d // 2, 2)
    x = d // 4
    yl = m // NZ
    z = lax.rem(m, NZ)

    z_dev = [(d, yl * NZ + lax.rem(z + 1, NZ)), (d, yl * NZ + lax.rem(z + NZ - 1, NZ))]
    y_dev = [(d, lax.rem(yl + k, NYL) * NZ + z) for k in (1, 2, 3)]
    x_dev = [
        (lax.rem(x + 1, NX) * 4 + yh * 2 + core, m),
        (lax.rem(x + NX - 1, NX) * 4 + yh * 2 + core, m),
    ]
    core_dev = (d + 1 - 2 * core, m)
    far_dev = (x * 4 + (1 - yh) * 2 + core, m)

    load_w = pltpu.make_async_copy(w_hbm, w, w_sem)
    load_w.start()

    barrier = pltpu.get_barrier_semaphore()
    partners = z_dev + y_dev + x_dev + [core_dev, far_dev]
    for device in partners:
        pl.semaphore_signal(barrier, inc=1, device_id=device, device_id_type=MESH)
    pl.semaphore_wait(barrier, len(partners))

    lines = [yl, yl + 1 - 2 * lax.rem(yl, 2), 2 - yl // 2, 3 - 3 * (yl // 2)]

    def from_z(way, step):
        return lax.rem(z + 2 * NZ - step if way == 0 else z + step, NZ)

    def rows_a(way, last):
        if not last:
            return pl.ds(0, RA)
        return pl.ds(0, HA) if way == 0 else pl.ds(HA, RA - HA)

    def rows_b(way, last):
        if not last:
            return pl.ds(RA, SEQ - RA)
        return pl.ds(RA, HB) if way == 0 else pl.ds(RA + HB, SEQ - RA - HB)

    def za(way, step, k, mine=False, last=False):
        rows = rows_a(way, last)
        block = lines[k] * NZ + from_z(way, step - 1)
        src = tok.at[rows] if mine else got.at[block, rows]
        return rdma(src, got.at[block, rows], s_za.at[way, step - 1, k], r_za.at[way, step - 1, k], z_dev[way])

    def za_in(way, step, k, last=False):
        rows = rows_a(way, last)
        block = lines[k] * NZ + from_z(way, step)
        here = got.at[block, rows]
        return rdma(here, here, s_za.at[way, step - 1, k], r_za.at[way, step - 1, k], z_dev[way])

    def zb(way, step, mine=False, last=False):
        rows = rows_b(way, last)
        block = yl * NZ + from_z(way, step - 1)
        src = tok.at[rows] if mine else got.at[block, rows]
        return rdma(src, got.at[block, rows], s_zb.at[way, step - 1], r_zb.at[way, step - 1], z_dev[way])

    def zb_in(way, step, last=False):
        rows = rows_b(way, last)
        here = got.at[yl * NZ + from_z(way, step), rows]
        return rdma(here, here, s_zb.at[way, step - 1], r_zb.at[way, step - 1], z_dev[way])

    def yb(k, slot, way, step, mine=False, last=False):
        rows = rows_b(way, last)
        block = yl * NZ + from_z(way, step)
        src = tok.at[rows] if mine else got.at[block, rows]
        return rdma(src, got.at[block, rows], s_yb.at[k, slot], r_yb.at[k, slot], y_dev[k])

    def yb_in(k, slot, way, step, last=False):
        rows = rows_b(way, last)
        here = got.at[lax.rem(yl + NYL - 1 - k, NYL) * NZ + from_z(way, step), rows]
        return rdma(here, here, s_yb.at[k, slot], r_yb.at[k, slot], y_dev[k])

    def ya(k):
        rows = pl.ds(0, RA)
        return rdma(tok.at[rows], got.at[m, rows], s_ya.at[k], r_ya.at[k], y_dev[k])

    for way in (0, 1):
        za(way, 1, 0, mine=True).start()
    for k in range(3):
        ya(k).start()
    for way in (0, 1):
        zb(way, 1, mine=True).start()
    for k in range(3):
        yb(k, 0, 0, 0, mine=True).start()

    here = tok[...]
    got[m] = here
    wide = here.astype(F32)
    middle = jnp.mean(wide, axis=1, keepdims=True)
    shift[...] = jnp.broadcast_to(middle, (SEQ, HD))
    moved = wide - middle
    total[...] = moved
    square[...] = moved * moved

    def add_rows(blocks, start, size):
        rows = pl.ds(start, size)
        base = shift[rows]
        first = total[rows]
        second = square[rows]
        for block in blocks:
            v = got[block, rows].astype(F32) - base
            first += v
            second += v * v
        total[rows] = first
        square[rows] = second

    def add_a(blocks):
        for start in range(0, RA, 64):
            add_rows(blocks, start, 64)

    def add_b(blocks):
        add_rows(blocks, RA, SEQ - RA)

    for k in (1, 2, 3):
        line = lines[k]
        at = lax.rem(yl - line + NYL, NYL) - 1
        rows = pl.ds(0, RA)
        ref = got.at[line * NZ + z, rows]
        rdma(ref, ref, s_ya.at[at], r_ya.at[at], z_dev[0]).wait_recv()
        for way in (0, 1):
            za(way, 1, k).start()
    add_a([lines[k] * NZ + z for k in (1, 2, 3)])

    def y_in(slots, far=False):
        blocks = []
        for slot, way, step in slots:
            for k in range(3):
                yb_in(k, slot, way, step, last=far).wait_recv()
                blocks.append(lax.rem(yl + NYL - 1 - k, NYL) * NZ + from_z(way, step))
        return blocks

    def pass_on(step, last):
        for k in range(4):
            for way in (0, 1):
                za_in(way, step, k).wait_recv()
                za(way, step + 1, k, last=last).start()
        for way in (0, 1):
            zb_in(way, step).wait_recv()
            zb(way, step + 1, last=last).start()
        for way in (0, 1):
            for k in range(3):
                yb(k, 2 * step - 1 + way, way, step).start()
        add_a([lines[k] * NZ + from_z(way, step) for k in range(4) for way in (0, 1)])
        add_b([yl * NZ + from_z(way, step) for way in (0, 1)])

    pass_on(1, False)
    add_b(y_in([(0, 0, 0)]))

    def middle_step(step, carry):
        pass_on(step, False)
        add_b(y_in([(2 * step - 3 + way, way, step - 1) for way in (0, 1)]))
        return carry

    lax.fori_loop(2, FAR - 1, middle_step, 0)
    pass_on(FAR - 1, True)
    add_b(y_in([(2 * FAR - 5 + way, way, FAR - 2) for way in (0, 1)]))
    for way in (0, 1):
        zb_in(way, FAR, last=True).wait_recv()
        for k in range(3):
            yb(k, 2 * FAR - 1 + way, way, FAR, last=True).start()
    for k in range(4):
        for way in (0, 1):
            za_in(way, FAR, k, last=True).wait_recv()
    far_z = from_z(0, FAR)
    add_a([lines[k] * NZ + far_z for k in range(4)])
    add_b([yl * NZ + far_z])
    add_b(y_in([(2 * FAR - 3 + way, way, FAR - 1) for way in (0, 1)]))
    blocks = y_in([(2 * FAR - 1, 0, FAR)], far=True)
    y_in([(2 * FAR, 1, FAR)], far=True)
    add_b(blocks)

    mean_moved = jnp.sum(total[...], axis=1, keepdims=True) / WIDTH
    spread = jnp.sum(square[...], axis=1, keepdims=True) / WIDTH - mean_moved * mean_moved
    total[...] = shift[...] + mean_moved
    square[...] = jnp.broadcast_to(lax.rsqrt(spread + 1e-06), (SEQ, HD))
    load_w.wait()

    def norm_copy(p):
        return rdma(normed.at[2 * p + 1 - core], other.at[p], s_n.at[p], r_n.at[p], core_dev)

    for p in range(GROUPS // 2):
        center = total[...]
        scale = square[...]
        pieces = []
        for group in (2 * p + 1 - core, 2 * p + core):
            for b in range(3):
                block = 3 * group + b
                v = (got[block].astype(F32) - center) * scale * gain[block]
                v = v.astype(BF16)
                normed[group, :, b * HD : (b + 1) * HD] = v
                pieces.append(v)
        norm_copy(p).start()
        left = jnp.concatenate(pieces, axis=1)
        right = jnp.concatenate([w[2 * p + 1 - core], w[2 * p + core]], axis=0)
        term = nn(left, right)
        if p == 0:
            proj[...] = term
        else:
            proj[...] += term

    score_scale = 1.0 / math.sqrt(HD)
    gain_q = jnp.broadcast_to(q_gain[...], (HD, HD)).T
    gain_k = jnp.broadcast_to(k_gain[...], (HD, HD)).T
    gain_q = jnp.concatenate([gain_q, gain_q], axis=1)
    gain_k = jnp.concatenate([gain_k, gain_k], axis=1)
    up_t = d_attn[...].astype(F32).T.astype(BF16)
    q_t = proj[:, 0:HD].T
    k_t = proj[:, HD : 2 * HD].T
    values = proj[:, 2 * HD :].astype(BF16)
    q_hat, q_inv = head_norm(q_t)
    k_hat, k_inv = head_norm(k_t)
    q_n_t = (q_hat * gain_q).astype(BF16)
    k_n_f = k_hat * gain_k
    k_n_t = k_n_f.astype(BF16)
    k_n = k_n_f.T.astype(BF16)
    scores = nn(k_n, q_n_t) * score_scale
    grad_prob = nn(values, up_t)
    raised = jnp.exp(scores - jnp.max(scores, axis=0, keepdims=True))
    probs = raised / jnp.sum(raised, axis=0, keepdims=True)
    probs_low = probs.astype(BF16)
    grad_score = probs * (grad_prob - jnp.sum(probs * grad_prob, axis=0, keepdims=True))
    grad_score = (grad_score * score_scale).astype(BF16)
    grad_v = nt(up_t, probs_low)
    grad_kn = nt(q_n_t, grad_score)
    grad_qn = nn(k_n_t, grad_score)
    joined[0:HD] = head_norm_back(grad_qn, q_hat, q_inv, gain_q).astype(BF16)
    joined[HD : 2 * HD] = head_norm_back(grad_kn, k_hat, k_inv, gain_k).astype(BF16)
    joined[2 * HD :] = grad_v.astype(BF16)
    send_j = rdma(joined, joined_other, s_j.at[0], r_j.at[0], core_dev)
    send_j.start()
    for p in range(GROUPS // 2):
        norm_copy(p).wait_recv()
    send_j.wait_recv()

    def grad_part(x_to, y_to, half):
        rows = pl.ds(half * HALF, HALF)
        left = jnp.concatenate([joined[rows], joined_other[rows]], axis=1)
        at = x_to * 2 + y_to
        right = jnp.concatenate([normed[at * 2 + core], other[at]], axis=0)
        return nn(left, right)

    def x_copy(i, way, kind):
        return rdma(sx.at[i, way, kind], rx.at[i, way, kind], s_x.at[i, way, kind], r_x.at[i, way, kind], x_dev[way])

    x_next = [lax.rem(x + 1, NX), lax.rem(x + NX - 1, NX)]
    x_far = lax.rem(x + 2, NX)

    def first_parts(i, y_to, send):
        for way in (0, 1):
            sx[i, way, 0] = grad_part(x_far, y_to, way).astype(BF16)
            if send:
                x_copy(i, way, 0).start()
        for way in (0, 1):
            sx[i, way, 1] = grad_part(x_next[way], y_to, 1 - way).astype(BF16)
            if send:
                x_copy(i, way, 1).start()

    def later_parts(i, y_to):
        for way in (0, 1):
            part[i, way] = grad_part(x_next[way], y_to, way)
        for half in (0, 1):
            own[i, half] = grad_part(x, y_to, half)

    def relay(i):
        for way in (0, 1):
            x_copy(i, way, 0).wait_recv()
            sx[i, way, 2] = (part[i, way] + rx[i, way, 0].astype(F32)).astype(BF16)
            x_copy(i, way, 2).start()

    def gather_half(i, half):
        x_copy(i, 1 - half, 1).wait_recv()
        x_copy(i, half, 2).wait_recv()
        return own[i, half] + rx[i, 1 - half, 1].astype(F32) + rx[i, half, 2].astype(F32)

    def y_copy(half):
        return rdma(sy.at[half], ry.at[half], s_y.at[half], r_y.at[half], far_dev)

    first_parts(0, 1 - yh, True)
    later_parts(0, 1 - yh)
    first_parts(1, yh, False)
    later_parts(1, yh)
    relay(0)
    for kind in (0, 1):
        for way in (0, 1):
            x_copy(1, way, kind).start()
    for half in (0, 1):
        sy[half] = gather_half(0, half).astype(BF16)
        y_copy(half).start()
    relay(1)

    for way in (0, 1):
        for k in range(4):
            for step in range(1, FAR + 1):
                za(way, step, k, last=step == FAR).wait_send()
        for step in range(1, FAR + 1):
            zb(way, step, last=step == FAR).wait_send()
    for k in range(3):
        ya(k).wait_send()
        yb(k, 0, 0, 0, mine=True).wait_send()
        for step in range(1, FAR + 1):
            for way in (0, 1):
                yb(k, 2 * step - 1 + way, way, step, last=step == FAR).wait_send()
    for p in range(GROUPS // 2):
        norm_copy(p).wait_send()
    send_j.wait_send()

    for half in (0, 1):
        own[1, half] = gather_half(1, half)
    for half in (0, 1):
        y_copy(half).wait_recv()
        final = own[1, half] + ry[half].astype(F32)
        out[:, half * HALF : (half + 1) * HALF] = final.T.astype(BF16)
    for i in (0, 1):
        for way in (0, 1):
            for kind in (0, 1, 2):
                x_copy(i, way, kind).wait_send()
    for half in (0, 1):
        y_copy(half).wait_send()


def local(tokens, ln_gain, w_qkv, q_gain, k_gain, d_attn):
    dma = pltpu.SemaphoreType.DMA
    vmem = pl.BlockSpec(memory_space=pltpu.VMEM)
    steps = 2 * FAR + 1
    pairs = []
    for shape in ((2, FAR, 4), (3,), (2, FAR), (3, steps), (GROUPS // 2,), (1,), (2, 2, 3), (2,)):
        pairs += [dma(shape), dma(shape)]
    return pl.pallas_call(
        body,
        out_shape=jax.ShapeDtypeStruct((COLS, COLS), BF16),
        in_specs=[vmem, vmem, pl.BlockSpec(memory_space=pl.ANY), vmem, vmem, vmem],
        out_specs=vmem,
        scratch_shapes=[
            pltpu.VMEM((BLOCKS, SEQ, HD), BF16),
            pltpu.VMEM((GROUPS, SEQ, COLS), BF16),
            pltpu.VMEM((GROUPS // 2, SEQ, COLS), BF16),
            pltpu.VMEM((GROUPS, COLS, COLS), BF16),
            pltpu.VMEM((SEQ, HD), F32),
            pltpu.VMEM((SEQ, HD), F32),
            pltpu.VMEM((SEQ, HD), F32),
            pltpu.VMEM((SEQ, COLS), F32),
            pltpu.VMEM((COLS, SEQ), BF16),
            pltpu.VMEM((COLS, SEQ), BF16),
            pltpu.VMEM((2, 2, HALF, COLS), F32),
            pltpu.VMEM((2, 2, HALF, COLS), F32),
            pltpu.VMEM((2, 2, 3, HALF, COLS), BF16),
            pltpu.VMEM((2, 2, 3, HALF, COLS), BF16),
            pltpu.VMEM((2, HALF, COLS), BF16),
            pltpu.VMEM((2, HALF, COLS), BF16),
            dma(()),
        ] + pairs,
        compiler_params=pltpu.CompilerParams(
            collective_id=0, has_side_effects=True, vmem_limit_bytes=48 * 2**20
        ),
        cost_estimate=pl.CostEstimate(flops=2_600_000_000, bytes_accessed=10_000_000, transcendentals=100_000),
        name="layer",
    )(
        tokens, ln_gain.reshape(BLOCKS, 1, HD), w_qkv.reshape(GROUPS, COLS, COLS), q_gain, k_gain, d_attn
    )


def solution(mesh):
    placed = (P("dp", "mp"), P(), P(None, "mp"), P("mp", None), P("mp", None), P("dp", "mp"))
    return jax.shard_map(
        local, mesh=mesh, in_specs=placed, out_specs=P("dp", "mp"), check_vma=False
    )
```

time: 350 us -> 95.9 us (0.27)
  waiting for transfers between devices: 318 us -> 0 us
  Pallas kernels: 0 us -> 88.8 us
  between operations: 13.5 us -> 0.02 us
  matrix products: 10.7 us -> 0 us
  other arithmetic: 7.85 us -> 0 us
  local copies, waits for them, and re-layouts: 0.32 us -> 6.78 us
    all_gather x1 -> x0, waiting for transfers between devices: 174 us -> none  [local(): gathered = lax.all_gather(tokens, 'mp', axis=1, tiled=True)]
    reduce_scatter x1 -> x0, waiting for transfers between devices: 143 us -> none  [local(): lax.psum_scatter(contract(normed, joined).astype(jnp.bfloat16), 'dp', sca...]
    pallas_call x0 -> x1, Pallas kernels: none -> 88.8 us  [local(): pl.pallas_call(body, out_shape=jax.ShapeDtypeStruct((COLS, COLS), BF16),...]
    dot_general x7 -> x0, matrix products: 10.7 us -> none  [the longest x1 4.85 us: contract(): jnp.einsum('rd,rc->dc', normed, gradient, preferred_element_type=jnp.floa...]
    unnamed x16 -> x13, local copies, waits for them, and re-layouts: 0.32 us -> 6.78 us
    reduce_sum x6 -> x0, other arithmetic: 4.28 us -> none  [the longest x1 2.54 us: norm_rows(): center = jnp.mean(widened, axis=-1, keepdims=True)]
  transfers between devices with their start and end apart: 2 -> 0, of which waited for: 2 -> 0; matrix products, arithmetic and copies ran while one was open for 0% -> 0% of each run, Pallas kernels for 0% -> 0%
where the time goes in v1:
time: 95.9 us; the launch traced here: 95.6 us
  Pallas kernels  88.8 us (93%)
  local copies, waits for them, and re-layouts  6.78 us (7%)
    pallas_call x1, Pallas kernels, local(): pl.pallas_call(body, out_shape=jax.ShapeDtypeStruct((COLS, COLS), BF16),...  88.8 us
    unnamed x13, local copies, waits for them, and re-layouts  6.78 us

profile of v1, /device:TPU:1, one launch (start us, length us, event | category | flops | bytes accessed | tf_op | source)
XLA Modules:
  0.0 95.6 jit_solution(8304062322528664430)
XLA Ops:
  0.0 0.0 copy-start
  0.0 2.3 %copy-done = bf16[6144,384]{1,0:T(8,128)(2,1)S(1)} copy-done((bf16[6144,384]{1,0:T(8,128)(2,1)S(1)}, bf16[6144,384]{1,0:T(8,128)(2,1)}, u32[]{:S(2)}) %copy-start) | copy-done | bytes 4718616
  2.3 0.0 copy-start.1
  2.3 0.8 copy-done.1
  3.2 0.0 copy-start.2
  3.2 0.8 copy-done.2
  4.0 0.0 copy-start.3
  4.0 0.7 copy-done.3
  4.8 0.0 copy-start.4
  4.8 0.7 copy-done.4
  5.4 0.0 copy-start.5
  5.4 0.7 copy-done.5
  6.1 88.8 %layer.1 = bf16[384,384]{1,0:T(8,128)(2,1)S(1)} custom-call(bf16[256,128]{1,0:T(8,128)(2,1)S(1)} %copy-done.1, f32[48,1,128]{2,1,0:T(1,128)S(1)} %bitcast.3, bf16[16,384,384]{2,1,0:T(8,128)(2,1)S(1)} %bitcast.2, f32[1,128]{1,0:T(1,128)S(1)} %copy-done.4, f32[1,128]{1,0:T(1,128)S(1)} %copy-done.5, bf16[256,128]{1,0:T(8,128)(2,1)S(1)} %copy-done.2), custom_call_target="tpu_custom_call" | custom-call | flops 2600000000 | bytes 10000000 | tf_op jit(solution)/shard_map/layer/pallas_call | solution.py:395
  94.9 0.7 copy.8
Async XLA Ops:
  0.0 2.3 %copy-start = (bf16[6144,384]{1,0:T(8,128)(2,1)S(1)}, bf16[6144,384]{1,0:T(8,128)(2,1)}, u32[]{:S(2)}) copy-start(bf16[6144,384]{1,0:T(8,128)(2,1)} %param.8) | copy-start | bytes 14155780
  2.3 0.8 copy-start.1
  3.2 0.8 copy-start.2
  4.0 0.7 copy-start.3
  4.8 0.7 copy-start.4
  5.4 0.7 copy-start.5

commit v2 on v0

v2 whole, which is shorter than its diff:
```python
import math

import jax
import jax.numpy as jnp
from jax import lax
from jax.experimental import pallas as pl
from jax.experimental.pallas import tpu as pltpu
from jax.sharding import PartitionSpec as P

MESH = pl.DeviceIdType.MESH
F32 = jnp.float32
BF16 = jnp.bfloat16
SEQ = 256
HD = 128
NX = 4
NYL = 4
NZ = 12
BLOCKS = NYL * NZ
WIDTH = BLOCKS * HD
COLS = 3 * HD
SLOTS = NZ // 2
FAR = NZ // 2
RA = 160
HA = RA // 2
HB = (SEQ - RA) // 2
HALF = COLS // 2
QUARTER = COLS // 4


def rdma(src, dst, send, recv, device):
    return pltpu.make_async_remote_copy(
        src_ref=src, dst_ref=dst, send_sem=send, recv_sem=recv, device_id=device, device_id_type=MESH
    )


def head_norm(t):
    center = jnp.mean(t, axis=0, keepdims=True)
    moved = t - center
    spread = jnp.mean(moved * moved, axis=0, keepdims=True)
    inverse = lax.rsqrt(spread + 1e-06)
    return moved * inverse, inverse


def head_norm_back(grad, normal, inverse, gain):
    scaled = grad * gain
    first = jnp.mean(scaled, axis=0, keepdims=True)
    second = jnp.mean(scaled * normal, axis=0, keepdims=True)
    return inverse * (scaled - first - normal * second)


def nt(a, b):
    return lax.dot_general(a, b, (((1,), (1,)), ((), ())), preferred_element_type=F32)


def nn(a, b):
    return jnp.dot(a, b, preferred_element_type=F32)


def merge(parts, count):
    mean = sum(p[0:2] for p in parts) / len(parts)
    spread = sum(p[2:4] for p in parts)
    moved = [p[0:2] - mean for p in parts]
    return mean, spread + count * sum(v * v for v in moved)


def body(
    tok, gain_in, w_in, q_gain_in, k_gain_in, d_attn_in, out,
    got, normed, other, w, gain, q_gain, k_gain, d_attn,
    stat, stat_y, stat_4, stat_z, center, scale, proj, joined, joined_other, up_t, gains_t,
    own, part, sx, rx, sy, ry, loads,
    s_za, r_za, s_ya, r_ya, s_zb, r_zb, s_yb, r_yb, s_sy, r_sy, s_sz, r_sz, s_n, r_n, s_j, r_j, s_x, r_x, s_y, r_y,
    s_yr,
):
    d = lax.axis_index("dp")
    m = lax.axis_index("mp")
    core = lax.rem(d, 2)
    yh = lax.rem(d // 2, 2)
    x = d // 4
    yl = m // NZ
    z = lax.rem(m, NZ)

    def z_at(hops):
        return (d, yl * NZ + lax.rem(z + hops, NZ))

    z_dev = [z_at(1), z_at(NZ - 1)]
    y_dev = [(d, lax.rem(yl + k, NYL) * NZ + z) for k in (1, 2, 3)]
    x_dev = [
        (lax.rem(x + 1, NX) * 4 + yh * 2 + core, m),
        (lax.rem(x + NX - 1, NX) * 4 + yh * 2 + core, m),
    ]
    core_dev = (d + 1 - 2 * core, m)
    far_dev = (x * 4 + (1 - yh) * 2 + core, m)

    def load(i, src, dst):
        return pltpu.make_async_copy(src, dst, loads.at[i])

    load_tok = load(0, tok, got.at[z, yl])
    load_w = load(1, w_in, w)
    small = [load(2, gain_in, gain), load(3, q_gain_in, q_gain), load(4, k_gain_in, k_gain), load(5, d_attn_in, d_attn)]
    load_tok.start()

    barrier = pltpu.get_barrier_semaphore()
    partners = [z_at(hops) for hops in range(1, NZ)] + y_dev + x_dev + [core_dev, far_dev]
    for device in partners:
        pl.semaphore_signal(barrier, inc=1, device_id=device, device_id_type=MESH)

    load_tok.wait()
    for copy in small:
        copy.start()
    load_w.start()
    turned = got[z, yl].astype(F32).T
    mean = jnp.mean(turned, axis=0, keepdims=True)
    moved = turned - mean
    spread = jnp.sum(moved * moved, axis=0, keepdims=True)
    stat[0:1] = mean[:, :HD]
    stat[1:2] = mean[:, HD:]
    stat[2:3] = spread[:, :HD]
    stat[3:4] = spread[:, HD:]
    pl.semaphore_wait(barrier, len(partners))

    lines = [yl, yl + 1 - 2 * lax.rem(yl, 2), 2 - yl // 2, 3 - 3 * (yl // 2)]

    def from_z(way, step):
        return lax.rem(z + 2 * NZ - step if way == 0 else z + step, NZ)

    def rows_a(way, step):
        if step < FAR:
            return pl.ds(0, RA)
        return pl.ds(0, HA) if way == 0 else pl.ds(HA, RA - HA)

    def rows_b(way, step):
        if step < FAR:
            return pl.ds(RA, SEQ - RA)
        return pl.ds(RA, HB) if way == 0 else pl.ds(RA + HB, SEQ - RA - HB)

    def za(way, step, k):
        rows = rows_a(way, step)
        at = from_z(way, step - 1)
        src = tok.at[rows] if step == 1 and k == 0 else got.at[at, lines[k], rows]
        return rdma(src, got.at[at, lines[k], rows], s_za.at[way, step - 1, k], r_za.at[way, step - 1, k], z_dev[way])

    def za_in(way, step, k):
        here = got.at[from_z(way, step), lines[k], rows_a(way, step)]
        return rdma(here, here, s_za.at[way, step - 1, k], r_za.at[way, step - 1, k], z_dev[way])

    def zb(way, step):
        rows = rows_b(way, step)
        at = from_z(way, step - 1)
        src = tok.at[rows] if step == 1 else got.at[at, yl, rows]
        return rdma(src, got.at[at, yl, rows], s_zb.at[way, step - 1], r_zb.at[way, step - 1], z_dev[way])

    def zb_in(way, step):
        here = got.at[from_z(way, step), yl, rows_b(way, step)]
        return rdma(here, here, s_zb.at[way, step - 1], r_zb.at[way, step - 1], z_dev[way])

    def slot_of(way, step):
        return 2 * step - 1 + way if step else 0

    def yb(k, way, step):
        rows = rows_b(way, step)
        at = from_z(way, step)
        slot = slot_of(way, step)
        src = tok.at[rows] if step == 0 else got.at[at, yl, rows]
        return rdma(src, got.at[at, yl, rows], s_yb.at[k, slot], r_yb.at[k, slot], y_dev[k])

    def yb_in(k, way, step):
        slot = slot_of(way, step)
        here = got.at[from_z(way, step), lax.rem(yl + NYL - 1 - k, NYL), rows_b(way, step)]
        return rdma(here, here, s_yb.at[k, slot], r_yb.at[k, slot], y_dev[k])

    def yb_relay(way, step):
        slot = slot_of(way, step)
        here = got.at[from_z(way, step), lax.rem(yl + 2, NYL), rows_b(way, step)]
        return rdma(here, here, s_yr.at[slot], r_yb.at[2 * (yl - 1), slot], (d, 3 * (yl - 1) * NZ + z))

    inner = jnp.logical_and(yl > 0, yl < NYL - 1)

    def each_yb(way, step, act):
        act(yb(1, way, step))

        @pl.when(yl < NYL - 1)
        def _():
            act(yb(0, way, step))

        @pl.when(yl > 0)
        def _():
            act(yb(2, way, step))

    def start(copy):
        copy.start()

    def wait_send(copy):
        copy.wait_send()

    def ya(k):
        rows = pl.ds(0, RA)
        at = lax.rem(lines[k] - yl + NYL, NYL) - 1
        return rdma(tok.at[rows], got.at[z, yl, rows], s_ya.at[at], r_ya.at[at], (d, lines[k] * NZ + z))

    def ya_in(k):
        at = lax.rem(yl - lines[k] + NYL, NYL) - 1
        here = got.at[z, lines[k], pl.ds(0, RA)]
        return rdma(here, here, s_ya.at[at], r_ya.at[at], z_dev[0])

    def stat_y_copy(k):
        return rdma(stat, stat_y.at[k], s_sy.at[k], r_sy.at[k], y_dev[k])

    def stat_z_copy(hops):
        return rdma(stat_4, stat_z.at[hops - 1], s_sz.at[hops - 1], r_sz.at[hops - 1], z_at(hops))

    for k in range(3):
        stat_y_copy(k).start()
    for way in (0, 1):
        za(way, 1, 0).start()
    for k in (1, 2, 3):
        ya(k).start()
    for way in (0, 1):
        zb(way, 1).start()
    each_yb(0, 0, start)

    for k in range(3):
        stat_y_copy(k).wait_recv()
    mean, spread = merge([stat[...]] + [stat_y[k] for k in range(3)], HD)
    stat_4[0:2] = mean
    stat_4[2:4] = spread
    for hops in range(1, NZ):
        stat_z_copy(hops).start()

    def z_pass(step, k):
        for way in (0, 1):
            za_in(way, step, k).wait_recv()
            if step < FAR:
                za(way, step + 1, k).start()

    def b_pass(step):
        for way in (0, 1):
            zb_in(way, step).wait_recv()
            if step < FAR:
                zb(way, step + 1).start()
            each_yb(way, step, start)

    def y_in(step):
        for way in (0, 1) if step else (0,):
            yb_in(1, way, step).wait_recv()

            @pl.when(inner)
            def _():
                yb_relay(way, step).start()

        for way in (0, 1) if step else (0,):
            for k in (0, 2):
                yb_in(k, way, step).wait_recv()

    def swap(zz):
        slot = zz // 6 * 3 + lax.rem(zz, 3)
        return rdma(normed.at[zz], other.at[slot], s_n.at[slot], r_n.at[slot], core_dev)

    def process(step):
        places = [from_z(way, step) for way in (0, 1)]
        if step == 0 or step == FAR:
            places = places[:1]
        middle = center[...]
        factor = scale[...]
        left, right = [], []
        for zz in places:
            for line in range(NYL):
                block = line * NZ + zz
                v = (got[zz, line].astype(F32) - middle) * factor * gain[block]
                v = v.astype(BF16)
                normed[zz, line] = v
                left.append(v)
                right.append(w[block])
        term = nn(jnp.concatenate(left, axis=1), jnp.concatenate(right, axis=0))
        if step == 0:
            proj[...] = term
        else:
            proj[...] += term
        for zz in places:

            @pl.when(lax.rem(zz // 3, 2) != core)
            def _():
                swap(zz).start()

    b_pass(1)
    z_pass(1, 0)
    for k in (1, 2, 3):
        ya_in(k).wait_recv()
        for way in (0, 1):
            za(way, 1, k).start()
    b_pass(2)
    y_in(0)
    for copy in small:
        copy.wait()
    for i, ref in enumerate((q_gain, k_gain)):
        column = jnp.broadcast_to(ref[...], (HD, HD)).T
        gains_t[i] = jnp.concatenate([column, column], axis=1)
    up_t[...] = d_attn[...].astype(F32).T.astype(BF16)

    b_pass(3)
    z_pass(2, 0)
    for k in (1, 2, 3):
        z_pass(1, k)
    b_pass(4)
    y_in(1)
    for hops in range(1, NZ):
        stat_z_copy(hops).wait_recv()
    mean, spread = merge([stat_4[...]] + [stat_z[hops - 1] for hops in range(1, NZ)], NYL * HD)
    factor = lax.rsqrt(spread / WIDTH + 1e-06)
    for i in (0, 1):
        rows = pl.ds(i * HD, HD)
        center[rows] = jnp.broadcast_to(mean[i : i + 1], (HD, HD)).T
        scale[rows] = jnp.broadcast_to(factor[i : i + 1], (HD, HD)).T
    load_w.wait()
    process(0)

    b_pass(5)
    z_pass(3, 0)
    for k in (1, 2, 3):
        z_pass(2, k)
    b_pass(6)
    y_in(2)
    process(1)
    y_in(3)

    z_pass(4, 0)
    for k in (1, 2, 3):
        z_pass(3, k)
    y_in(4)
    process(2)
    z_pass(5, 0)
    for k in (1, 2, 3):
        z_pass(4, k)
    y_in(5)
    process(3)
    z_pass(6, 0)
    for k in (1, 2, 3):
        z_pass(5, k)
    process(4)
    y_in(6)
    process(5)
    for k in (1, 2, 3):
        z_pass(6, k)
    process(6)

    score_scale = 1.0 / math.sqrt(HD)
    gain_q = gains_t[0]
    gain_k = gains_t[1]
    q_t = proj[:, 0:HD].T
    k_t = proj[:, HD : 2 * HD].T
    values = proj[:, 2 * HD :].astype(BF16)
    q_hat, q_inv = head_norm(q_t)
    k_hat, k_inv = head_norm(k_t)
    q_n_t = (q_hat * gain_q).astype(BF16)
    k_n_f = k_hat * gain_k
    k_n_t = k_n_f.astype(BF16)
    k_n = k_n_f.T.astype(BF16)
    scores = nn(k_n, q_n_t) * score_scale
    grad_prob = nn(values, up_t[...])
    raised = jnp.exp(scores - jnp.max(scores, axis=0, keepdims=True))
    probs = raised / jnp.sum(raised, axis=0, keepdims=True)
    probs_low = probs.astype(BF16)
    grad_score = probs * (grad_prob - jnp.sum(probs * grad_prob, axis=0, keepdims=True))
    grad_score = (grad_score * score_scale).astype(BF16)
    grad_v = nt(up_t[...], probs_low)
    grad_kn = nt(q_n_t, grad_score)
    grad_qn = nn(k_n_t, grad_score)
    joined[0:HD] = head_norm_back(grad_qn, q_hat, q_inv, gain_q).astype(BF16)
    joined[HD : 2 * HD] = head_norm_back(grad_kn, k_hat, k_inv, gain_k).astype(BF16)
    joined[2 * HD :] = grad_v.astype(BF16)
    send_j = rdma(joined, joined_other, s_j.at[0], r_j.at[0], core_dev)
    send_j.start()

    def swap_in(slot):
        return rdma(other.at[slot], other.at[slot], s_n.at[slot], r_n.at[slot], core_dev)

    for slot in range(SLOTS):
        swap_in(slot).wait_recv()
    send_j.wait_recv()

    def grad_part(x_to, y_to, half):
        rows = pl.ds(half * HALF, HALF)
        left = jnp.concatenate([joined[rows], joined_other[rows]], axis=1)
        mine = jnp.concatenate([normed[3 * (2 * y_to + core) + b, x_to] for b in range(3)], axis=1)
        theirs = jnp.concatenate([other[3 * y_to + b, x_to] for b in range(3)], axis=1)
        return nn(left, jnp.concatenate([mine, theirs], axis=0))

    x_next = [lax.rem(x + 1, NX), lax.rem(x + NX - 1, NX)]
    x_far = lax.rem(x + 2, NX)

    def x_copy(i, way, kind, q):
        at = (i, way, kind, q)
        return rdma(sx.at[at], rx.at[at], s_x.at[at], r_x.at[at], x_dev[way])

    def put(i, way, kind, value):
        value = value.astype(BF16)
        for q in (0, 1):
            sx[i, way, kind, q] = value[q * QUARTER : (q + 1) * QUARTER]

    def x_start(i, kind, q):
        for way in (0, 1):
            x_copy(i, way, kind, q).start()

    def relay(i, q):
        for way in (0, 1):
            x_copy(i, way, 0, q).wait_recv()
            sx[i, way, 2, q] = (part[i, way, q] + rx[i, way, 0, q].astype(F32)).astype(BF16)
            x_copy(i, way, 2, q).start()

    def later_parts(i, y_to):
        for way in (0, 1):
            value = grad_part(x_next[way], y_to, way)
            for q in (0, 1):
                part[i, way, q] = value[q * QUARTER : (q + 1) * QUARTER]
        for half in (0, 1):
            value = grad_part(x, y_to, half)
            for q in (0, 1):
                own[i, half, q] = value[q * QUARTER : (q + 1) * QUARTER]

    def gathered(i, half, q):
        x_copy(i, 1 - half, 1, q).wait_recv()
        x_copy(i, half, 2, q).wait_recv()
        return own[i, half, q] + rx[i, 1 - half, 1, q].astype(F32) + rx[i, half, 2, q].astype(F32)

    def y_copy(half, q):
        at = (half, q)
        return rdma(sy.at[at], ry.at[at], s_y.at[at], r_y.at[at], far_dev)

    def y_start(q):
        for half in (0, 1):
            sy[half, q] = gathered(0, half, q).astype(BF16)
            y_copy(half, q).start()

    for way in (0, 1):
        put(0, way, 0, grad_part(x_far, 1 - yh, way))
        x_copy(0, way, 0, 0).start()
    for way in (0, 1):
        put(0, way, 1, grad_part(x_next[way], 1 - yh, 1 - way))
        x_copy(0, way, 1, 0).start()
    x_start(0, 0, 1)
    later_parts(0, 1 - yh)
    for way in (0, 1):
        put(1, way, 0, grad_part(x_far, yh, way))
        put(1, way, 1, grad_part(x_next[way], yh, 1 - way))
    relay(0, 0)
    x_start(0, 1, 1)
    later_parts(1, yh)
    relay(0, 1)
    x_start(1, 0, 0)
    x_start(1, 1, 0)
    x_start(1, 0, 1)
    y_start(0)
    relay(1, 0)
    x_start(1, 1, 1)
    y_start(1)
    relay(1, 1)

    for way in (0, 1):
        for k in range(4):
            for step in range(1, FAR + 1):
                za(way, step, k).wait_send()
        for step in range(1, FAR + 1):
            zb(way, step).wait_send()
    for k in (1, 2, 3):
        ya(k).wait_send()
    for k in range(3):
        stat_y_copy(k).wait_send()
    for hops in range(1, NZ):
        stat_z_copy(hops).wait_send()
    arrivals = [(0, 0)] + [(way, step) for step in range(1, FAR + 1) for way in (0, 1)]
    for way, step in arrivals:
        yb(1, way, step).wait_send()

    @pl.when(yl < NYL - 1)
    def _():
        for way, step in arrivals:
            yb(0, way, step).wait_send()

    @pl.when(yl > 0)
    def _():
        for way, step in arrivals:
            yb(2, way, step).wait_send()

    @pl.when(inner)
    def _():
        for way, step in arrivals:
            yb_relay(way, step).wait_send()

    for slot in range(SLOTS):
        swap_in(slot).wait_send()
    send_j.wait_send()

    final = []
    for half in (0, 1):
        for q in (0, 1):
            value = gathered(1, half, q)
            y_copy(half, q).wait_recv()
            final.append(value + ry[half, q].astype(F32))
    final = jnp.concatenate(final, axis=0)
    for b in range(3):
        out[:, b * HD : (b + 1) * HD] = final[b * HD : (b + 1) * HD].T.astype(BF16)
    for i in (0, 1):
        for way in (0, 1):
            for kind in (0, 1, 2):
                for q in (0, 1):
                    x_copy(i, way, kind, q).wait_send()
    for half in (0, 1):
        for q in (0, 1):
            y_copy(half, q).wait_send()


def local(tokens, ln_gain, w_qkv, q_gain, k_gain, d_attn):
    dma = pltpu.SemaphoreType.DMA
    hbm = pl.BlockSpec(memory_space=pltpu.HBM)
    steps = 2 * FAR + 1
    pairs = []
    for shape in (
        (2, FAR, 4), (3,), (2, FAR), (3, steps), (3,), (NZ - 1,), (SLOTS,), (1,), (2, 2, 3, 2), (2, 2),
    ):
        pairs += [dma(shape), dma(shape)]
    return pl.pallas_call(
        body,
        out_shape=jax.ShapeDtypeStruct((COLS, COLS), BF16),
        in_specs=[hbm] * 6,
        out_specs=pl.BlockSpec(memory_space=pltpu.VMEM),
        scratch_shapes=[
            pltpu.VMEM((NZ, NYL, SEQ, HD), BF16),
            pltpu.VMEM((NZ, NYL, SEQ, HD), BF16),
            pltpu.VMEM((SLOTS, NYL, SEQ, HD), BF16),
            pltpu.VMEM((BLOCKS, HD, COLS), BF16),
            pltpu.VMEM((BLOCKS, 1, HD), F32),
            pltpu.VMEM((1, HD), F32),
            pltpu.VMEM((1, HD), F32),
            pltpu.VMEM((SEQ, HD), BF16),
            pltpu.VMEM((4, HD), F32),
            pltpu.VMEM((3, 4, HD), F32),
            pltpu.VMEM((4, HD), F32),
            pltpu.VMEM((NZ - 1, 4, HD), F32),
            pltpu.VMEM((SEQ, HD), F32),
            pltpu.VMEM((SEQ, HD), F32),
            pltpu.VMEM((SEQ, COLS), F32),
            pltpu.VMEM((COLS, SEQ), BF16),
            pltpu.VMEM((COLS, SEQ), BF16),
            pltpu.VMEM((HD, SEQ), BF16),
            pltpu.VMEM((2, HD, SEQ), F32),
            pltpu.VMEM((2, 2, 2, QUARTER, COLS), F32),
            pltpu.VMEM((2, 2, 2, QUARTER, COLS), F32),
            pltpu.VMEM((2, 2, 3, 2, QUARTER, COLS), BF16),
            pltpu.VMEM((2, 2, 3, 2, QUARTER, COLS), BF16),
            pltpu.VMEM((2, 2, QUARTER, COLS), BF16),
            pltpu.VMEM((2, 2, QUARTER, COLS), BF16),
            dma((6,)),
        ] + pairs + [dma((steps,))],
        compiler_params=pltpu.CompilerParams(
            collective_id=0, has_side_effects=True, vmem_limit_bytes=60 * 2**20
        ),
        cost_estimate=pl.CostEstimate(flops=2_600_000_000, bytes_accessed=10_000_000, transcendentals=100_000),
        name="layer",
    )(
        tokens, ln_gain.reshape(BLOCKS, 1, HD), w_qkv.reshape(BLOCKS, HD, COLS), q_gain, k_gain, d_attn
    )


def solution(mesh):
    placed = (P("dp", "mp"), P(), P(None, "mp"), P("mp", None), P("mp", None), P("dp", "mp"))
    return jax.shard_map(
        local, mesh=mesh, in_specs=placed, out_specs=P("dp", "mp"), check_vma=False
    )
```

time: 350 us -> 87.4 us (0.25)
  waiting for transfers between devices: 318 us -> 0 us
  Pallas kernels: 0 us -> 85.5 us
  between operations: 13.5 us -> 0.01 us
  matrix products: 10.7 us -> 0 us
  other arithmetic: 7.85 us -> 0 us
    all_gather x1 -> x0, waiting for transfers between devices: 174 us -> none  [local(): gathered = lax.all_gather(tokens, 'mp', axis=1, tiled=True)]
    reduce_scatter x1 -> x0, waiting for transfers between devices: 143 us -> none  [local(): lax.psum_scatter(contract(normed, joined).astype(jnp.bfloat16), 'dp', sca...]
    pallas_call x0 -> x1, Pallas kernels: none -> 85.5 us  [local(): pl.pallas_call(body, out_shape=jax.ShapeDtypeStruct((COLS, COLS), BF16),...]
    dot_general x7 -> x0, matrix products: 10.7 us -> none  [the longest x1 4.85 us: contract(): jnp.einsum('rd,rc->dc', normed, gradient, preferred_element_type=jnp.floa...]
    reduce_sum x6 -> x0, other arithmetic: 4.28 us -> none  [the longest x1 2.54 us: norm_rows(): center = jnp.mean(widened, axis=-1, keepdims=True)]
  transfers between devices with their start and end apart: 2 -> 0, of which waited for: 2 -> 0; matrix products, arithmetic and copies ran while one was open for 0% -> 0% of each run, Pallas kernels for 0% -> 0%
where the time goes in v2:
time: 87.4 us; the launch traced here: 87.2 us
  Pallas kernels  85.5 us (98%)
  local copies, waits for them, and re-layouts  1.71 us (2%)
    pallas_call x1, Pallas kernels, local(): pl.pallas_call(body, out_shape=jax.ShapeDtypeStruct((COLS, COLS), BF16),...  85.5 us

profile of v2, /device:TPU:1, one launch (start us, length us, event | category | flops | bytes accessed | tf_op | source)
XLA Modules:
  0.0 87.2 jit_solution(15910433014307436056)
XLA Ops:
  0.0 85.5 %layer.1 = bf16[384,384]{1,0:T(8,128)(2,1)} custom-call(bf16[256,128]{1,0:T(8,128)(2,1)} %tok.1, f32[48,1,128]{2,1,0:T(1,128)} %bitcast.3, bf16[48,128,384]{2,1,0:T(8,128)(2,1)} %bitcast.2, f32[1,128]{1,0:T(1,128)} %q_gain_in.1, f32[1,128]{1,0:T(1,128)} %k_gain_in.1, bf16[256,128]{1,0:T(8,128)(2,1)} %d_attn_in.1), custom_call_target="tpu_custom_call" | custom-call | flops 2600000000 | bytes 10000000 | tf_op jit(solution)/shard_map/layer/pallas_call | solution.py:520
  85.5 1.7 %copy.8 = bf16[384,384]{1,0:T(8,128)(2,1)} copy(bf16[384,384]{1,0:T(8,128)(2,1)} %layer.1) | data formatting | bytes 589824

commit v3 on v2

--- a/solution.py
+++ b/solution.py
@@ -20,9 +20,9 @@
 COLS = 3 * HD
 SLOTS = NZ // 2
 FAR = NZ // 2
-RA = 160
-HA = RA // 2
-HB = (SEQ - RA) // 2
+RA = 176
+HA = 96
+HB = 48
 HALF = COLS // 2
 QUARTER = COLS // 4
 
@@ -56,20 +56,12 @@
     return jnp.dot(a, b, preferred_element_type=F32)
 
 
-def merge(parts, count):
-    mean = sum(p[0:2] for p in parts) / len(parts)
-    spread = sum(p[2:4] for p in parts)
-    moved = [p[0:2] - mean for p in parts]
-    return mean, spread + count * sum(v * v for v in moved)
-
-
 def body(
     tok, gain_in, w_in, q_gain_in, k_gain_in, d_attn_in, out,
-    got, normed, other, w, gain, q_gain, k_gain, d_attn,
-    stat, stat_y, stat_4, stat_z, center, scale, proj, joined, joined_other, up_t, gains_t,
+    got, other, w, gain, q_gain, k_gain, d_attn,
+    shift, total, square, joined, joined_other, mean_own, mean_other, drift, up_t, gains_t,
     own, part, sx, rx, sy, ry, loads,
-    s_za, r_za, s_ya, r_ya, s_zb, r_zb, s_yb, r_yb, s_sy, r_sy, s_sz, r_sz, s_n, r_n, s_j, r_j, s_x, r_x, s_y, r_y,
-    s_yr,
+    s_za, r_za, s_ya, r_ya, s_zb, r_zb, s_yb, r_yb, s_n, r_n, s_m, r_m, s_j, r_j, s_x, r_x, s_y, r_y,
 ):
     d = lax.axis_index("dp")
     m = lax.axis_index("mp")
@@ -79,10 +71,7 @@
     yl = m // NZ
     z = lax.rem(m, NZ)
 
-    def z_at(hops):
-        return (d, yl * NZ + lax.rem(z + hops, NZ))
-
-    z_dev = [z_at(1), z_at(NZ - 1)]
+    z_dev = [(d, yl * NZ + lax.rem(z + hops, NZ)) for hops in (1, NZ - 1)]
     y_dev = [(d, lax.rem(yl + k, NYL) * NZ + z) for k in (1, 2, 3)]
     x_dev = [
         (lax.rem(x + 1, NX) * 4 + yh * 2 + core, m),
@@ -98,24 +87,15 @@
     load_w = load(1, w_in, w)
     small = [load(2, gain_in, gain), load(3, q_gain_in, q_gain), load(4, k_gain_in, k_gain), load(5, d_attn_in, d_attn)]
     load_tok.start()
-
-    barrier = pltpu.get_barrier_semaphore()
-    partners = [z_at(hops) for hops in range(1, NZ)] + y_dev + x_dev + [core_dev, far_dev]
-    for device in partners:
-        pl.semaphore_signal(barrier, inc=1, device_id=device, device_id_type=MESH)
-
-    load_tok.wait()
     for copy in small:
         copy.start()
     load_w.start()
-    turned = got[z, yl].astype(F32).T
-    mean = jnp.mean(turned, axis=0, keepdims=True)
-    moved = turned - mean
-    spread = jnp.sum(moved * moved, axis=0, keepdims=True)
-    stat[0:1] = mean[:, :HD]
-    stat[1:2] = mean[:, HD:]
-    stat[2:3] = spread[:, :HD]
-    stat[3:4] = spread[:, HD:]
+
+    barrier = pltpu.get_barrier_semaphore()
+    partners = z_dev + y_dev + x_dev + [core_dev, far_dev]
+    for device in partners:
+        pl.semaphore_signal(barrier, inc=1, device_id=device, device_id_type=MESH)
+
     pl.semaphore_wait(barrier, len(partners))
 
     lines = [yl, yl + 1 - 2 * lax.rem(yl, 2), 2 - yl // 2, 3 - 3 * (yl // 2)]
@@ -168,29 +148,12 @@
         here = got.at[from_z(way, step), lax.rem(yl + NYL - 1 - k, NYL), rows_b(way, step)]
         return rdma(here, here, s_yb.at[k, slot], r_yb.at[k, slot], y_dev[k])
 
-    def yb_relay(way, step):
-        slot = slot_of(way, step)
-        here = got.at[from_z(way, step), lax.rem(yl + 2, NYL), rows_b(way, step)]
-        return rdma(here, here, s_yr.at[slot], r_yb.at[2 * (yl - 1), slot], (d, 3 * (yl - 1) * NZ + z))
-
-    inner = jnp.logical_and(yl > 0, yl < NYL - 1)
-
     def each_yb(way, step, act):
-        act(yb(1, way, step))
-
-        @pl.when(yl < NYL - 1)
-        def _():
-            act(yb(0, way, step))
-
-        @pl.when(yl > 0)
-        def _():
-            act(yb(2, way, step))
+        for k in range(3):
+            act(yb(k, way, step))
 
     def start(copy):
         copy.start()
-
-    def wait_send(copy):
-        copy.wait_send()
 
     def ya(k):
         rows = pl.ds(0, RA)
@@ -202,14 +165,6 @@
         here = got.at[z, lines[k], pl.ds(0, RA)]
         return rdma(here, here, s_ya.at[at], r_ya.at[at], z_dev[0])
 
-    def stat_y_copy(k):
-        return rdma(stat, stat_y.at[k], s_sy.at[k], r_sy.at[k], y_dev[k])
-
-    def stat_z_copy(hops):
-        return rdma(stat_4, stat_z.at[hops - 1], s_sz.at[hops - 1], r_sz.at[hops - 1], z_at(hops))
-
-    for k in range(3):
-        stat_y_copy(k).start()
     for way in (0, 1):
         za(way, 1, 0).start()
     for k in (1, 2, 3):
@@ -218,13 +173,8 @@
         zb(way, 1).start()
     each_yb(0, 0, start)
 
-    for k in range(3):
-        stat_y_copy(k).wait_recv()
-    mean, spread = merge([stat[...]] + [stat_y[k] for k in range(3)], HD)
-    stat_4[0:2] = mean
-    stat_4[2:4] = spread
-    for hops in range(1, NZ):
-        stat_z_copy(hops).start()
+    load_tok.wait()
+    shift[...] = jnp.broadcast_to(jnp.mean(got[z, yl].astype(F32), axis=1, keepdims=True), (SEQ, HD))
 
     def z_pass(step, k):
         for way in (0, 1):
@@ -241,113 +191,95 @@
 
     def y_in(step):
         for way in (0, 1) if step else (0,):
-            yb_in(1, way, step).wait_recv()
-
-            @pl.when(inner)
-            def _():
-                yb_relay(way, step).start()
-
-        for way in (0, 1) if step else (0,):
-            for k in (0, 2):
+            for k in range(3):
                 yb_in(k, way, step).wait_recv()
 
     def swap(zz):
         slot = zz // 6 * 3 + lax.rem(zz, 3)
-        return rdma(normed.at[zz], other.at[slot], s_n.at[slot], r_n.at[slot], core_dev)
-
-    def process(step):
-        places = [from_z(way, step) for way in (0, 1)]
-        if step == 0 or step == FAR:
-            places = places[:1]
-        middle = center[...]
-        factor = scale[...]
-        left, right = [], []
-        for zz in places:
-            for line in range(NYL):
-                block = line * NZ + zz
-                v = (got[zz, line].astype(F32) - middle) * factor * gain[block]
-                v = v.astype(BF16)
-                normed[zz, line] = v
-                left.append(v)
-                right.append(w[block])
-        term = nn(jnp.concatenate(left, axis=1), jnp.concatenate(right, axis=0))
-        if step == 0:
-            proj[...] = term
-        else:
-            proj[...] += term
-        for zz in places:
-
-            @pl.when(lax.rem(zz // 3, 2) != core)
-            def _():
-                swap(zz).start()
-
-    b_pass(1)
-    z_pass(1, 0)
-    for k in (1, 2, 3):
-        ya_in(k).wait_recv()
-        for way in (0, 1):
-            za(way, 1, k).start()
-    b_pass(2)
-    y_in(0)
-    for copy in small:
-        copy.wait()
-    for i, ref in enumerate((q_gain, k_gain)):
-        column = jnp.broadcast_to(ref[...], (HD, HD)).T
-        gains_t[i] = jnp.concatenate([column, column], axis=1)
-    up_t[...] = d_attn[...].astype(F32).T.astype(BF16)
-
-    b_pass(3)
-    z_pass(2, 0)
-    for k in (1, 2, 3):
-        z_pass(1, k)
-    b_pass(4)
-    y_in(1)
-    for hops in range(1, NZ):
-        stat_z_copy(hops).wait_recv()
-    mean, spread = merge([stat_4[...]] + [stat_z[hops - 1] for hops in range(1, NZ)], NYL * HD)
-    factor = lax.rsqrt(spread / WIDTH + 1e-06)
-    for i in (0, 1):
-        rows = pl.ds(i * HD, HD)
-        center[rows] = jnp.broadcast_to(mean[i : i + 1], (HD, HD)).T
-        scale[rows] = jnp.broadcast_to(factor[i : i + 1], (HD, HD)).T
+        return rdma(got.at[zz], other.at[slot], s_n.at[slot], r_n.at[slot], core_dev)
+
+    def process(zz, first):
+        base = shift[...]
+        one = jnp.zeros((SEQ, HD), F32) if first else total[...]
+        two = jnp.zeros((SEQ, HD), F32) if first else square[...]
+        for line in range(NYL):
+            v = got[zz, line].astype(F32) - base
+            one += v
+            two += v * v
+        total[...] = one
+        square[...] = two
+
+        @pl.when(lax.rem(zz // 3, 2) != core)
+        def _():
+            swap(zz).start()
+
+    ready = []
+    count = [0]
+
+    def work():
+        if ready:
+            process(ready.pop(0), count[0] == 0)
+            count[0] += 1
+
+    for turn in range(1, FAR + 2):
+        if turn <= FAR:
+            b_pass(turn)
+            z_pass(turn, 0)
+        for k in (1, 2, 3):
+            if turn == 1:
+                ya_in(k).wait_recv()
+                for way in (0, 1):
+                    za(way, 1, k).start()
+            else:
+                z_pass(turn - 1, k)
+            work()
+        if turn == 1:
+            for copy in small:
+                copy.wait()
+            for i, ref in enumerate((q_gain, k_gain)):
+                column = jnp.broadcast_to(ref[...], (HD, HD)).T
+                gains_t[i] = jnp.concatenate([column, column], axis=1)
+            up_t[...] = d_attn[...].astype(F32).T.astype(BF16)
+        if turn >= 2:
+            step = turn - 2
+            y_in(step)
+            ready += [from_z(way, step) for way in ((0, 1) if step else (0,))]
+    while len(ready) > 1:
+        work()
+    y_in(FAR)
+    ready.append(from_z(0, FAR))
+    while ready:
+        work()
+
+    moved = jnp.sum(total[...], axis=1, keepdims=True) / WIDTH
+    spread = jnp.sum(square[...], axis=1, keepdims=True) / WIDTH - moved * moved
+    mean = shift[:, 0:1] + moved
+    rstd = lax.rsqrt(spread + 1e-06)
+    mean_t = jnp.broadcast_to(mean, (SEQ, HD)).T
+    rstd_t = jnp.broadcast_to(rstd, (SEQ, HD)).T
+    mean_own[...] = mean_t[0:8]
+    send_m = rdma(mean_own, mean_other, s_m.at[0], r_m.at[0], core_dev)
+    send_m.start()
+    total[...] = jnp.broadcast_to(mean, (SEQ, HD))
+    square[...] = jnp.broadcast_to(rstd, (SEQ, HD))
     load_w.wait()
-    process(0)
-
-    b_pass(5)
-    z_pass(3, 0)
-    for k in (1, 2, 3):
-        z_pass(2, k)
-    b_pass(6)
-    y_in(2)
-    process(1)
-    y_in(3)
-
-    z_pass(4, 0)
-    for k in (1, 2, 3):
-        z_pass(3, k)
-    y_in(4)
-    process(2)
-    z_pass(5, 0)
-    for k in (1, 2, 3):
-        z_pass(4, k)
-    y_in(5)
-    process(3)
-    z_pass(6, 0)
-    for k in (1, 2, 3):
-        z_pass(5, k)
-    process(4)
-    y_in(6)
-    process(5)
-    for k in (1, 2, 3):
-        z_pass(6, k)
-    process(6)
+    projected = None
+    for first in range(0, BLOCKS, 8):
+        left = []
+        for block in range(first, first + 8):
+            v = got[block % NZ, block // NZ].astype(F32)
+            v = (v - total[...]) * square[...] * gain[block : block + 1]
+            left.append(v.astype(BF16))
+        right = w[first : first + 8].reshape(8 * HD, COLS)
+        term = nn(jnp.concatenate(left, axis=1), right)
+        projected = term if projected is None else projected + term
 
     score_scale = 1.0 / math.sqrt(HD)
     gain_q = gains_t[0]
     gain_k = gains_t[1]
-    q_t = proj[:, 0:HD].T
-    k_t = proj[:, HD : 2 * HD].T
-    values = proj[:, 2 * HD :].astype(BF16)
+    q_t = projected[:, 0:HD].T
+    k_t = projected[:, HD : 2 * HD].T
+    values = projected[:, 2 * HD :].astype(BF16)
     q_hat, q_inv = head_norm(q_t)
     k_hat, k_inv = head_norm(k_t)
     q_n_t = (q_hat * gain_q).astype(BF16)
@@ -357,16 +289,16 @@
     scores = nn(k_n, q_n_t) * score_scale
     grad_prob = nn(values, up_t[...])
     raised = jnp.exp(scores - jnp.max(scores, axis=0, keepdims=True))
-    probs = raised / jnp.sum(raised, axis=0, keepdims=True)
+    probs = raised * (1.0 / jnp.sum(raised, axis=0, keepdims=True))
     probs_low = probs.astype(BF16)
     grad_score = probs * (grad_prob - jnp.sum(probs * grad_prob, axis=0, keepdims=True))
     grad_score = (grad_score * score_scale).astype(BF16)
     grad_v = nt(up_t[...], probs_low)
     grad_kn = nt(q_n_t, grad_score)
     grad_qn = nn(k_n_t, grad_score)
-    joined[0:HD] = head_norm_back(grad_qn, q_hat, q_inv, gain_q).astype(BF16)
-    joined[HD : 2 * HD] = head_norm_back(grad_kn, k_hat, k_inv, gain_k).astype(BF16)
-    joined[2 * HD :] = grad_v.astype(BF16)
+    joined[0:HD] = (rstd_t * head_norm_back(grad_qn, q_hat, q_inv, gain_q)).astype(BF16)
+    joined[HD : 2 * HD] = (rstd_t * head_norm_back(grad_kn, k_hat, k_inv, gain_k)).astype(BF16)
+    joined[2 * HD :] = (rstd_t * grad_v).astype(BF16)
     send_j = rdma(joined, joined_other, s_j.at[0], r_j.at[0], core_dev)
     send_j.start()
 
@@ -375,14 +307,20 @@
 
     for slot in range(SLOTS):
         swap_in(slot).wait_recv()
+    send_m.wait_recv()
     send_j.wait_recv()
+    off = joined[...].astype(F32) * mean_own[0:1] + joined_other[...].astype(F32) * mean_other[0:1]
+    drift[...] = jnp.broadcast_to(jnp.sum(off, axis=1, keepdims=True), (COLS, HD))
 
     def grad_part(x_to, y_to, half):
         rows = pl.ds(half * HALF, HALF)
         left = jnp.concatenate([joined[rows], joined_other[rows]], axis=1)
-        mine = jnp.concatenate([normed[3 * (2 * y_to + core) + b, x_to] for b in range(3)], axis=1)
+        mine = jnp.concatenate([got[3 * (2 * y_to + core) + b, x_to] for b in range(3)], axis=1)
         theirs = jnp.concatenate([other[3 * y_to + b, x_to] for b in range(3)], axis=1)
-        return nn(left, jnp.concatenate([mine, theirs], axis=0))
+        value = nn(left, jnp.concatenate([mine, theirs], axis=0))
+        group = [gain[pl.ds(x_to * NZ + 3 * (2 * y_to + core) + b, 1)] for b in range(3)]
+        away = drift[rows]
+        return (value - jnp.concatenate([away] * 3, axis=1)) * jnp.concatenate(group, axis=1)
 
     x_next = [lax.rem(x + 1, NX), lax.rem(x + NX - 1, NX)]
     x_far = lax.rem(x + 2, NX)
@@ -463,30 +401,13 @@
     for k in (1, 2, 3):
         ya(k).wait_send()
     for k in range(3):
-        stat_y_copy(k).wait_send()
-    for hops in range(1, NZ):
-        stat_z_copy(hops).wait_send()
-    arrivals = [(0, 0)] + [(way, step) for step in range(1, FAR + 1) for way in (0, 1)]
-    for way, step in arrivals:
-        yb(1, way, step).wait_send()
-
-    @pl.when(yl < NYL - 1)
-    def _():
-        for way, step in arrivals:
-            yb(0, way, step).wait_send()
-
-    @pl.when(yl > 0)
-    def _():
-        for way, step in arrivals:
-            yb(2, way, step).wait_send()
-
-    @pl.when(inner)
-    def _():
-        for way, step in arrivals:
-            yb_relay(way, step).wait_send()
-
+        yb(k, 0, 0).wait_send()
+        for step in range(1, FAR + 1):
+            for way in (0, 1):
+                yb(k, way, step).wait_send()
     for slot in range(SLOTS):
         swap_in(slot).wait_send()
+    send_m.wait_send()
     send_j.wait_send()
 
     final = []
@@ -514,7 +435,7 @@
     steps = 2 * FAR + 1
     pairs = []
     for shape in (
-        (2, FAR, 4), (3,), (2, FAR), (3, steps), (3,), (NZ - 1,), (SLOTS,), (1,), (2, 2, 3, 2), (2, 2),
+        (2, FAR, 4), (3,), (2, FAR), (3, steps), (SLOTS,), (1,), (1,), (2, 2, 3, 2), (2, 2),
     ):
         pairs += [dma(shape), dma(shape)]
     return pl.pallas_call(
@@ -524,22 +445,20 @@
         out_specs=pl.BlockSpec(memory_space=pltpu.VMEM),
         scratch_shapes=[
             pltpu.VMEM((NZ, NYL, SEQ, HD), BF16),
-            pltpu.VMEM((NZ, NYL, SEQ, HD), BF16),
             pltpu.VMEM((SLOTS, NYL, SEQ, HD), BF16),
             pltpu.VMEM((BLOCKS, HD, COLS), BF16),
-            pltpu.VMEM((BLOCKS, 1, HD), F32),
+            pltpu.VMEM((BLOCKS, HD), F32),
             pltpu.VMEM((1, HD), F32),
             pltpu.VMEM((1, HD), F32),
             pltpu.VMEM((SEQ, HD), BF16),
-            pltpu.VMEM((4, HD), F32),
-            pltpu.VMEM((3, 4, HD), F32),
-            pltpu.VMEM((4, HD), F32),
-            pltpu.VMEM((NZ - 1, 4, HD), F32),
             pltpu.VMEM((SEQ, HD), F32),
             pltpu.VMEM((SEQ, HD), F32),
-            pltpu.VMEM((SEQ, COLS), F32),
+            pltpu.VMEM((SEQ, HD), F32),
             pltpu.VMEM((COLS, SEQ), BF16),
             pltpu.VMEM((COLS, SEQ), BF16),
+            pltpu.VMEM((8, SEQ), F32),
+            pltpu.VMEM((8, SEQ), F32),
+            pltpu.VMEM((COLS, HD), F32),
             pltpu.VMEM((HD, SEQ), BF16),
             pltpu.VMEM((2, HD, SEQ), F32),
             pltpu.VMEM((2, 2, 2, QUARTER, COLS), F32),
@@ -549,14 +468,19 @@
             pltpu.VMEM((2, 2, QUARTER, COLS), BF16),
             pltpu.VMEM((2, 2, QUARTER, COLS), BF16),
             dma((6,)),
-        ] + pairs + [dma((steps,))],
+        ] + pairs,
         compiler_params=pltpu.CompilerParams(
-            collective_id=0, has_side_effects=True, vmem_limit_bytes=60 * 2**20
+            collective_id=0, has_side_effects=True, vmem_limit_bytes=48 * 2**20
         ),
         cost_estimate=pl.CostEstimate(flops=2_600_000_000, bytes_accessed=10_000_000, transcendentals=100_000),
         name="layer",
     )(
-        tokens, ln_gain.reshape(BLOCKS, 1, HD), w_qkv.reshape(BLOCKS, HD, COLS), q_gain, k_gain, d_attn
+        *(
+            pltpu.with_memory_space_constraint(array, pltpu.HBM)
+            for array in (
+                tokens, ln_gain.reshape(BLOCKS, HD), w_qkv.reshape(BLOCKS, HD, COLS), q_gain, k_gain, d_attn
+            )
+        )
     )
 
 

time: 87.4 us -> 82.6 us (0.945)
  Pallas kernels: 85.5 us -> 81.7 us
  local copies, waits for them, and re-layouts: 1.71 us -> 0.72 us
    pallas_call x1, Pallas kernels: 85.5 us -> 81.7 us  [local(): pl.pallas_call(body, out_shape=jax.ShapeDtypeStruct((COLS, COLS), BF16),...]
    unnamed x1, local copies, waits for them, and re-layouts: 1.71 us -> 0.72 us
where the time goes in v3:
time: 82.6 us; the launch traced here: 82.5 us
  Pallas kernels  81.7 us (99%)
    pallas_call x1, Pallas kernels, local(): pl.pallas_call(body, out_shape=jax.ShapeDtypeStruct((COLS, COLS), BF16),...  81.7 us

profile of v3, /device:TPU:1, one launch (start us, length us, event | category | flops | bytes accessed | tf_op | source)
XLA Modules:
  0.0 82.5 jit_solution(7857835075085877971)
XLA Ops:
  0.0 81.7 %layer.1 = bf16[384,384]{1,0:T(8,128)(2,1)S(1)} custom-call(bf16[256,128]{1,0:T(8,128)(2,1)} %tok.1, f32[48,128]{1,0:T(8,128)} %bitcast.3, bf16[48,128,384]{2,1,0:T(8,128)(2,1)} %bitcast.2, f32[1,128]{1,0:T(1,128)} %q_gain_in.1, f32[1,128]{1,0:T(1,128)} %k_gain_in.1, bf16[256,128]{1,0:T(8,128)(2,1)} %d_attn_in.1), custom_call_target="tpu_custom_call" | custom-call | flops 2600000000 | bytes 10000000 | tf_op jit(solution)/shard_map/layer/pallas_call | solution.py:441
  81.8 0.7 copy.8

commit v4 on v3

--- a/solution.py
+++ b/solution.py
@@ -20,11 +20,28 @@
 COLS = 3 * HD
 SLOTS = NZ // 2
 FAR = NZ // 2
-RA = 176
-HA = 96
+RA = 160
+HA = 80
 HB = 48
 HALF = COLS // 2
-QUARTER = COLS // 4
+CUTS = (4, 2)
+
+
+ORDER = (
+    ("a", 0, 1, 0), ("a", 1, 1, 0), ("b", 0, 1, 0), ("b", 1, 1, 0), ("l", 0, 0, 1), ("l", 0, 0, 2),
+    ("a", 0, 2, 0), ("a", 1, 2, 0), ("b", 1, 2, 0), ("b", 0, 2, 0), ("l", 0, 0, 3), ("a", 0, 1, 1),
+    ("a", 0, 1, 2), ("a", 1, 1, 1), ("a", 1, 1, 2), ("b", 1, 3, 0), ("b", 0, 3, 0), ("a", 0, 1, 3),
+    ("a", 1, 1, 3), ("a", 0, 2, 1), ("a", 0, 3, 0), ("a", 1, 2, 1), ("a", 1, 2, 2), ("a", 1, 3, 0),
+    ("a", 0, 2, 2), ("a", 0, 2, 3), ("a", 1, 2, 3), ("a", 0, 3, 1), ("y", 1, 1, 0), ("b", 0, 4, 0),
+    ("b", 1, 4, 0), ("y", 1, 2, 0), ("a", 1, 3, 1), ("y", 0, 1, 0), ("a", 0, 3, 2), ("a", 1, 3, 2),
+    ("a", 0, 3, 3), ("a", 1, 3, 3), ("a", 0, 4, 0), ("a", 1, 4, 0), ("b", 0, 5, 0), ("b", 1, 5, 0),
+    ("a", 0, 4, 1), ("y", 0, 0, 0), ("a", 1, 4, 1), ("a", 0, 4, 2), ("a", 0, 4, 3), ("a", 1, 4, 2),
+    ("y", 0, 4, 0), ("y", 0, 2, 0), ("a", 1, 4, 3), ("b", 1, 6, 0), ("a", 0, 5, 0), ("a", 1, 5, 0),
+    ("b", 0, 6, 0), ("a", 0, 5, 1), ("a", 1, 5, 1), ("a", 1, 5, 2), ("a", 0, 5, 2), ("a", 0, 5, 3),
+    ("a", 1, 5, 3), ("y", 1, 3, 0), ("a", 0, 6, 0), ("a", 1, 6, 1), ("y", 1, 5, 0), ("y", 0, 5, 0),
+    ("y", 0, 3, 0), ("y", 1, 4, 0), ("a", 0, 6, 1), ("y", 1, 6, 0), ("a", 1, 6, 0), ("y", 0, 6, 0),
+    ("a", 1, 6, 2), ("a", 0, 6, 2), ("a", 0, 6, 3), ("a", 1, 6, 3),
+)
 
 
 def rdma(src, dst, send, recv, device):
@@ -100,8 +117,17 @@
 
     lines = [yl, yl + 1 - 2 * lax.rem(yl, 2), 2 - yl // 2, 3 - 3 * (yl // 2)]
 
+    places = {(0, 0): z, (1, 0): z}
+    for step in range(1, FAR + 1):
+        places[0, step] = lax.rem(z + NZ - step, NZ)
+        places[1, step] = lax.rem(z + step, NZ) if step < FAR else places[0, FAR]
+    y_from = [lax.rem(yl + NYL - 1 - k, NYL) for k in range(3)]
+    line_out = [0] + [lax.rem(lines[k] - yl + NYL, NYL) - 1 for k in (1, 2, 3)]
+    line_in = [0] + [lax.rem(yl - lines[k] + NYL, NYL) - 1 for k in (1, 2, 3)]
+    line_dev = [None] + [(d, lines[k] * NZ + z) for k in (1, 2, 3)]
+
     def from_z(way, step):
-        return lax.rem(z + 2 * NZ - step if way == 0 else z + step, NZ)
+        return places[way, step]
 
     def rows_a(way, step):
         if step < FAR:
@@ -145,7 +171,7 @@
 
     def yb_in(k, way, step):
         slot = slot_of(way, step)
-        here = got.at[from_z(way, step), lax.rem(yl + NYL - 1 - k, NYL), rows_b(way, step)]
+        here = got.at[from_z(way, step), y_from[k], rows_b(way, step)]
         return rdma(here, here, s_yb.at[k, slot], r_yb.at[k, slot], y_dev[k])
 
     def each_yb(way, step, act):
@@ -157,11 +183,11 @@
 
     def ya(k):
         rows = pl.ds(0, RA)
-        at = lax.rem(lines[k] - yl + NYL, NYL) - 1
-        return rdma(tok.at[rows], got.at[z, yl, rows], s_ya.at[at], r_ya.at[at], (d, lines[k] * NZ + z))
+        at = line_out[k]
+        return rdma(tok.at[rows], got.at[z, yl, rows], s_ya.at[at], r_ya.at[at], line_dev[k])
 
     def ya_in(k):
-        at = lax.rem(yl - lines[k] + NYL, NYL) - 1
+        at = line_in[k]
         here = got.at[z, lines[k], pl.ds(0, RA)]
         return rdma(here, here, s_ya.at[at], r_ya.at[at], z_dev[0])
 
@@ -176,23 +202,25 @@
     load_tok.wait()
     shift[...] = jnp.broadcast_to(jnp.mean(got[z, yl].astype(F32), axis=1, keepdims=True), (SEQ, HD))
 
-    def z_pass(step, k):
+    def z_pass(way, step, k):
+        za_in(way, step, k).wait_recv()
+        if step < FAR:
+            za(way, step + 1, k).start()
+
+    def b_pass(way, step):
+        zb_in(way, step).wait_recv()
+        if step < FAR:
+            zb(way, step + 1).start()
+        each_yb(way, step, start)
+
+    def l_pass(k):
+        ya_in(k).wait_recv()
         for way in (0, 1):
-            za_in(way, step, k).wait_recv()
-            if step < FAR:
-                za(way, step + 1, k).start()
-
-    def b_pass(step):
-        for way in (0, 1):
-            zb_in(way, step).wait_recv()
-            if step < FAR:
-                zb(way, step + 1).start()
-            each_yb(way, step, start)
-
-    def y_in(step):
-        for way in (0, 1) if step else (0,):
-            for k in range(3):
-                yb_in(k, way, step).wait_recv()
+            za(way, 1, k).start()
+
+    def y_in(way, step):
+        for k in range(3):
+            yb_in(k, way, step).wait_recv()
 
     def swap(zz):
         slot = zz // 6 * 3 + lax.rem(zz, 3)
@@ -213,43 +241,40 @@
         def _():
             swap(zz).start()
 
+    needs = {(0, 0): {("l", 0, 0, k) for k in (1, 2, 3)} | {("y", 0, 0, 0)}}
+    for step in range(1, FAR + 1):
+        for way in (0, 1):
+            at = needs.setdefault((way if step < FAR else 0, step), set())
+            at |= {("a", way, step, k) for k in range(4)} | {("b", way, step, 0), ("y", way, step, 0)}
     ready = []
-    count = [0]
-
-    def work():
-        if ready:
-            process(ready.pop(0), count[0] == 0)
-            count[0] += 1
-
-    for turn in range(1, FAR + 2):
-        if turn <= FAR:
-            b_pass(turn)
-            z_pass(turn, 0)
-        for k in (1, 2, 3):
-            if turn == 1:
-                ya_in(k).wait_recv()
-                for way in (0, 1):
-                    za(way, 1, k).start()
-            else:
-                z_pass(turn - 1, k)
-            work()
-        if turn == 1:
+    fresh = True
+    for turn, item in enumerate(ORDER):
+        kind, way, step, k = item
+        if kind == "a":
+            z_pass(way, step, k)
+        elif kind == "b":
+            b_pass(way, step)
+        elif kind == "l":
+            l_pass(k)
+        else:
+            y_in(way, step)
+        for place, missing in needs.items():
+            if item in missing:
+                missing.remove(item)
+                if not missing:
+                    ready.append(place)
+        if turn == 5:
             for copy in small:
                 copy.wait()
             for i, ref in enumerate((q_gain, k_gain)):
                 column = jnp.broadcast_to(ref[...], (HD, HD)).T
                 gains_t[i] = jnp.concatenate([column, column], axis=1)
             up_t[...] = d_attn[...].astype(F32).T.astype(BF16)
-        if turn >= 2:
-            step = turn - 2
-            y_in(step)
-            ready += [from_z(way, step) for way in ((0, 1) if step else (0,))]
-    while len(ready) > 1:
-        work()
-    y_in(FAR)
-    ready.append(from_z(0, FAR))
-    while ready:
-        work()
+        if ready:
+            process(from_z(*ready.pop(0)), fresh)
+            fresh = False
+    for place in ready:
+        process(from_z(*place), False)
 
     moved = jnp.sum(total[...], axis=1, keepdims=True) / WIDTH
     spread = jnp.sum(square[...], axis=1, keepdims=True) / WIDTH - moved * moved
@@ -305,91 +330,110 @@
     def swap_in(slot):
         return rdma(other.at[slot], other.at[slot], s_n.at[slot], r_n.at[slot], core_dev)
 
+    x_next = [lax.rem(x + 1, NX), lax.rem(x + NX - 1, NX)]
+    x_far = lax.rem(x + 2, NX)
+
+    def half_rows(half):
+        return pl.ds(half * HALF, HALF)
+
+    def mine(x_to, y_to):
+        return jnp.concatenate([got[3 * (2 * y_to + core) + b, x_to] for b in range(3)], axis=1)
+
+    def theirs(x_to, y_to):
+        return jnp.concatenate([other[3 * y_to + b, x_to] for b in range(3)], axis=1)
+
+    def corrected(value, x_to, y_to, half):
+        group = [gain[pl.ds(x_to * NZ + 3 * (2 * y_to + core) + b, 1)] for b in range(3)]
+        away = drift[half_rows(half)]
+        return (value - jnp.concatenate([away] * 3, axis=1)) * jnp.concatenate(group, axis=1)
+
+    def grad_part(x_to, y_to, half):
+        rows = half_rows(half)
+        left = jnp.concatenate([joined[rows], joined_other[rows]], axis=1)
+        value = nn(left, jnp.concatenate([mine(x_to, y_to), theirs(x_to, y_to)], axis=0))
+        return corrected(value, x_to, y_to, half)
+
+    early = [nn(joined[half_rows(way)], mine(x_far, 1 - yh)) for way in (0, 1)]
+    off = jnp.sum(joined[...].astype(F32) * mean_own[0:1], axis=1, keepdims=True)
     for slot in range(SLOTS):
         swap_in(slot).wait_recv()
     send_m.wait_recv()
     send_j.wait_recv()
-    off = joined[...].astype(F32) * mean_own[0:1] + joined_other[...].astype(F32) * mean_other[0:1]
-    drift[...] = jnp.broadcast_to(jnp.sum(off, axis=1, keepdims=True), (COLS, HD))
-
-    def grad_part(x_to, y_to, half):
-        rows = pl.ds(half * HALF, HALF)
-        left = jnp.concatenate([joined[rows], joined_other[rows]], axis=1)
-        mine = jnp.concatenate([got[3 * (2 * y_to + core) + b, x_to] for b in range(3)], axis=1)
-        theirs = jnp.concatenate([other[3 * y_to + b, x_to] for b in range(3)], axis=1)
-        value = nn(left, jnp.concatenate([mine, theirs], axis=0))
-        group = [gain[pl.ds(x_to * NZ + 3 * (2 * y_to + core) + b, 1)] for b in range(3)]
-        away = drift[rows]
-        return (value - jnp.concatenate([away] * 3, axis=1)) * jnp.concatenate(group, axis=1)
-
-    x_next = [lax.rem(x + 1, NX), lax.rem(x + NX - 1, NX)]
-    x_far = lax.rem(x + 2, NX)
+    off += jnp.sum(joined_other[...].astype(F32) * mean_other[0:1], axis=1, keepdims=True)
+    drift[...] = jnp.broadcast_to(off, (COLS, HD))
+
+    def piece(i, q):
+        size = HALF // CUTS[i]
+        return pl.ds(q * size, size)
 
     def x_copy(i, way, kind, q):
-        at = (i, way, kind, q)
-        return rdma(sx.at[at], rx.at[at], s_x.at[at], r_x.at[at], x_dev[way])
-
-    def put(i, way, kind, value):
-        value = value.astype(BF16)
-        for q in (0, 1):
-            sx[i, way, kind, q] = value[q * QUARTER : (q + 1) * QUARTER]
+        at = (i, way, kind, piece(i, q))
+        sem = (i, way, kind, q)
+        return rdma(sx.at[at], rx.at[at], s_x.at[sem], r_x.at[sem], x_dev[way])
 
     def x_start(i, kind, q):
         for way in (0, 1):
             x_copy(i, way, kind, q).start()
 
     def relay(i, q):
+        rows = piece(i, q)
         for way in (0, 1):
             x_copy(i, way, 0, q).wait_recv()
-            sx[i, way, 2, q] = (part[i, way, q] + rx[i, way, 0, q].astype(F32)).astype(BF16)
+            sx[i, way, 2, rows] = (part[i, way, rows] + rx[i, way, 0, rows].astype(F32)).astype(BF16)
             x_copy(i, way, 2, q).start()
 
     def later_parts(i, y_to):
         for way in (0, 1):
-            value = grad_part(x_next[way], y_to, way)
-            for q in (0, 1):
-                part[i, way, q] = value[q * QUARTER : (q + 1) * QUARTER]
+            part[i, way] = grad_part(x_next[way], y_to, way)
         for half in (0, 1):
-            value = grad_part(x, y_to, half)
-            for q in (0, 1):
-                own[i, half, q] = value[q * QUARTER : (q + 1) * QUARTER]
+            own[i, half] = grad_part(x, y_to, half)
 
     def gathered(i, half, q):
+        rows = piece(i, q)
         x_copy(i, 1 - half, 1, q).wait_recv()
         x_copy(i, half, 2, q).wait_recv()
-        return own[i, half, q] + rx[i, 1 - half, 1, q].astype(F32) + rx[i, half, 2, q].astype(F32)
+        return own[i, half, rows] + rx[i, 1 - half, 1, rows].astype(F32) + rx[i, half, 2, rows].astype(F32)
 
     def y_copy(half, q):
-        at = (half, q)
-        return rdma(sy.at[at], ry.at[at], s_y.at[at], r_y.at[at], far_dev)
+        at = (half, piece(0, q))
+        return rdma(sy.at[at], ry.at[at], s_y.at[half, q], r_y.at[half, q], far_dev)
 
     def y_start(q):
         for half in (0, 1):
-            sy[half, q] = gathered(0, half, q).astype(BF16)
+            sy[half, piece(0, q)] = gathered(0, half, q).astype(BF16)
             y_copy(half, q).start()
 
     for way in (0, 1):
-        put(0, way, 0, grad_part(x_far, 1 - yh, way))
+        value = early[way] + nn(joined_other[half_rows(way)], theirs(x_far, 1 - yh))
+        sx[0, way, 0] = corrected(value, x_far, 1 - yh, way).astype(BF16)
         x_copy(0, way, 0, 0).start()
     for way in (0, 1):
-        put(0, way, 1, grad_part(x_next[way], 1 - yh, 1 - way))
+        sx[0, way, 1] = grad_part(x_next[way], 1 - yh, 1 - way).astype(BF16)
         x_copy(0, way, 1, 0).start()
     x_start(0, 0, 1)
+    x_start(0, 1, 1)
     later_parts(0, 1 - yh)
+    relay(0, 0)
+    x_start(0, 0, 2)
+    x_start(0, 1, 2)
     for way in (0, 1):
-        put(1, way, 0, grad_part(x_far, yh, way))
-        put(1, way, 1, grad_part(x_next[way], yh, 1 - way))
-    relay(0, 0)
-    x_start(0, 1, 1)
+        sx[1, way, 0] = grad_part(x_far, yh, way).astype(BF16)
+        sx[1, way, 1] = grad_part(x_next[way], yh, 1 - way).astype(BF16)
+    relay(0, 1)
+    x_start(0, 0, 3)
+    x_start(0, 1, 3)
+    y_start(0)
+    relay(0, 2)
+    x_start(1, 0, 0)
     later_parts(1, yh)
-    relay(0, 1)
-    x_start(1, 0, 0)
+    y_start(1)
+    relay(0, 3)
     x_start(1, 1, 0)
     x_start(1, 0, 1)
-    y_start(0)
+    y_start(2)
     relay(1, 0)
     x_start(1, 1, 1)
-    y_start(1)
+    y_start(3)
     relay(1, 1)
 
     for way in (0, 1):
@@ -412,20 +456,21 @@
 
     final = []
     for half in (0, 1):
-        for q in (0, 1):
-            value = gathered(1, half, q)
+        for q in range(CUTS[1]):
+            final.append(gathered(1, half, q))
+    for half in (0, 1):
+        for q in range(CUTS[0]):
             y_copy(half, q).wait_recv()
-            final.append(value + ry[half, q].astype(F32))
-    final = jnp.concatenate(final, axis=0)
+    final = jnp.concatenate(final, axis=0) + jnp.concatenate([ry[0], ry[1]], axis=0).astype(F32)
     for b in range(3):
         out[:, b * HD : (b + 1) * HD] = final[b * HD : (b + 1) * HD].T.astype(BF16)
     for i in (0, 1):
         for way in (0, 1):
             for kind in (0, 1, 2):
-                for q in (0, 1):
+                for q in range(CUTS[i]):
                     x_copy(i, way, kind, q).wait_send()
     for half in (0, 1):
-        for q in (0, 1):
+        for q in range(CUTS[0]):
             y_copy(half, q).wait_send()
 
 
@@ -435,7 +480,7 @@
     steps = 2 * FAR + 1
     pairs = []
     for shape in (
-        (2, FAR, 4), (3,), (2, FAR), (3, steps), (SLOTS,), (1,), (1,), (2, 2, 3, 2), (2, 2),
+        (2, FAR, 4), (3,), (2, FAR), (3, steps), (SLOTS,), (1,), (1,), (2, 2, 3, CUTS[0]), (2, CUTS[0]),
     ):
         pairs += [dma(shape), dma(shape)]
     return pl.pallas_call(
@@ -461,12 +506,12 @@
             pltpu.VMEM((COLS, HD), F32),
             pltpu.VMEM((HD, SEQ), BF16),
             pltpu.VMEM((2, HD, SEQ), F32),
-            pltpu.VMEM((2, 2, 2, QUARTER, COLS), F32),
-            pltpu.VMEM((2, 2, 2, QUARTER, COLS), F32),
-            pltpu.VMEM((2, 2, 3, 2, QUARTER, COLS), BF16),
-            pltpu.VMEM((2, 2, 3, 2, QUARTER, COLS), BF16),
-            pltpu.VMEM((2, 2, QUARTER, COLS), BF16),
-            pltpu.VMEM((2, 2, QUARTER, COLS), BF16),
+            pltpu.VMEM((2, 2, HALF, COLS), F32),
+            pltpu.VMEM((2, 2, HALF, COLS), F32),
+            pltpu.VMEM((2, 2, 3, HALF, COLS), BF16),
+            pltpu.VMEM((2, 2, 3, HALF, COLS), BF16),
+            pltpu.VMEM((2, HALF, COLS), BF16),
+            pltpu.VMEM((2, HALF, COLS), BF16),
             dma((6,)),
         ] + pairs,
         compiler_params=pltpu.CompilerParams(

time: 82.6 us -> 82.2 us (level)
  no operation moved by 1% of the time
where the time goes in v4:
time: 82.2 us; the launch traced here: 82.1 us
  Pallas kernels  81.4 us (99%)
    pallas_call x1, Pallas kernels, local(): pl.pallas_call(body, out_shape=jax.ShapeDtypeStruct((COLS, COLS), BF16),...  81.4 us

profile of v4, /device:TPU:1, one launch (start us, length us, event | category | flops | bytes accessed | tf_op | source)
XLA Modules:
  0.0 82.1 jit_solution(13352460420932988410)
XLA Ops:
  0.0 81.4 %layer.1 = bf16[384,384]{1,0:T(8,128)(2,1)S(1)} custom-call(bf16[256,128]{1,0:T(8,128)(2,1)} %tok.1, f32[48,128]{1,0:T(8,128)} %bitcast.3, bf16[48,128,384]{2,1,0:T(8,128)(2,1)} %bitcast.2, f32[1,128]{1,0:T(1,128)} %q_gain_in.1, f32[1,128]{1,0:T(1,128)} %k_gain_in.1, bf16[256,128]{1,0:T(8,128)(2,1)} %d_attn_in.1), custom_call_target="tpu_custom_call" | custom-call | flops 2600000000 | bytes 10000000 | tf_op jit(solution)/shard_map/layer/pallas_call | solution.py:486
  81.4 0.7 copy.8

commit v5 on v4

--- a/solution.py
+++ b/solution.py
@@ -28,19 +28,19 @@
 
 
 ORDER = (
-    ("a", 0, 1, 0), ("a", 1, 1, 0), ("b", 0, 1, 0), ("b", 1, 1, 0), ("l", 0, 0, 1), ("l", 0, 0, 2),
-    ("a", 0, 2, 0), ("a", 1, 2, 0), ("b", 1, 2, 0), ("b", 0, 2, 0), ("l", 0, 0, 3), ("a", 0, 1, 1),
-    ("a", 0, 1, 2), ("a", 1, 1, 1), ("a", 1, 1, 2), ("b", 1, 3, 0), ("b", 0, 3, 0), ("a", 0, 1, 3),
-    ("a", 1, 1, 3), ("a", 0, 2, 1), ("a", 0, 3, 0), ("a", 1, 2, 1), ("a", 1, 2, 2), ("a", 1, 3, 0),
-    ("a", 0, 2, 2), ("a", 0, 2, 3), ("a", 1, 2, 3), ("a", 0, 3, 1), ("y", 1, 1, 0), ("b", 0, 4, 0),
-    ("b", 1, 4, 0), ("y", 1, 2, 0), ("a", 1, 3, 1), ("y", 0, 1, 0), ("a", 0, 3, 2), ("a", 1, 3, 2),
-    ("a", 0, 3, 3), ("a", 1, 3, 3), ("a", 0, 4, 0), ("a", 1, 4, 0), ("b", 0, 5, 0), ("b", 1, 5, 0),
-    ("a", 0, 4, 1), ("y", 0, 0, 0), ("a", 1, 4, 1), ("a", 0, 4, 2), ("a", 0, 4, 3), ("a", 1, 4, 2),
-    ("y", 0, 4, 0), ("y", 0, 2, 0), ("a", 1, 4, 3), ("b", 1, 6, 0), ("a", 0, 5, 0), ("a", 1, 5, 0),
-    ("b", 0, 6, 0), ("a", 0, 5, 1), ("a", 1, 5, 1), ("a", 1, 5, 2), ("a", 0, 5, 2), ("a", 0, 5, 3),
-    ("a", 1, 5, 3), ("y", 1, 3, 0), ("a", 0, 6, 0), ("a", 1, 6, 1), ("y", 1, 5, 0), ("y", 0, 5, 0),
-    ("y", 0, 3, 0), ("y", 1, 4, 0), ("a", 0, 6, 1), ("y", 1, 6, 0), ("a", 1, 6, 0), ("y", 0, 6, 0),
-    ("a", 1, 6, 2), ("a", 0, 6, 2), ("a", 0, 6, 3), ("a", 1, 6, 3),
+    ("b", 0, 1, 0), ("b", 1, 1, 0), ("a", 0, 1, 0), ("a", 1, 1, 0), ("l", 0, 0, 1), ("l", 0, 0, 2),
+    ("l", 0, 0, 3), ("b", 0, 2, 0), ("b", 1, 2, 0), ("a", 0, 2, 0), ("a", 1, 2, 0), ("a", 0, 1, 1),
+    ("a", 1, 1, 1), ("a", 0, 1, 2), ("a", 1, 1, 2), ("a", 0, 1, 3), ("a", 1, 1, 3), ("y", 0, 0, 0),
+    ("b", 0, 3, 0), ("b", 1, 3, 0), ("a", 0, 3, 0), ("a", 1, 3, 0), ("a", 0, 2, 1), ("a", 1, 2, 1),
+    ("a", 0, 2, 2), ("a", 1, 2, 2), ("a", 0, 2, 3), ("a", 1, 2, 3), ("y", 0, 1, 0), ("y", 1, 1, 0),
+    ("b", 0, 4, 0), ("b", 1, 4, 0), ("a", 0, 4, 0), ("a", 1, 4, 0), ("a", 0, 3, 1), ("a", 1, 3, 1),
+    ("a", 0, 3, 2), ("a", 1, 3, 2), ("a", 0, 3, 3), ("a", 1, 3, 3), ("y", 0, 2, 0), ("y", 1, 2, 0),
+    ("b", 0, 5, 0), ("b", 1, 5, 0), ("a", 0, 5, 0), ("a", 1, 5, 0), ("a", 0, 4, 1), ("a", 1, 4, 1),
+    ("a", 0, 4, 2), ("a", 1, 4, 2), ("a", 0, 4, 3), ("a", 1, 4, 3), ("y", 0, 3, 0), ("y", 1, 3, 0),
+    ("b", 0, 6, 0), ("b", 1, 6, 0), ("a", 0, 6, 0), ("a", 1, 6, 0), ("a", 0, 5, 1), ("a", 1, 5, 1),
+    ("a", 0, 5, 2), ("a", 1, 5, 2), ("a", 0, 5, 3), ("a", 1, 5, 3), ("y", 0, 4, 0), ("y", 1, 4, 0),
+    ("a", 0, 6, 1), ("a", 1, 6, 1), ("a", 0, 6, 2), ("a", 1, 6, 2), ("a", 0, 6, 3), ("a", 1, 6, 3),
+    ("y", 0, 5, 0), ("y", 1, 5, 0), ("y", 0, 6, 0), ("y", 1, 6, 0),
 )
 
 

time: 82.2 us -> 81.3 us (0.989)
  Pallas kernels: 81.4 us -> 80.4 us
    pallas_call x1, Pallas kernels: 81.4 us -> 80.4 us  [local(): pl.pallas_call(body, out_shape=jax.ShapeDtypeStruct((COLS, COLS), BF16),...]
where the time goes in v5:
time: 81.3 us; the launch traced here: 81.2 us
  Pallas kernels  80.4 us (99%)
    pallas_call x1, Pallas kernels, local(): pl.pallas_call(body, out_shape=jax.ShapeDtypeStruct((COLS, COLS), BF16),...  80.4 us

profile of v5, /device:TPU:1, one launch (start us, length us, event | category | flops | bytes accessed | tf_op | source)
XLA Modules:
  0.0 81.2 jit_solution(5687812675444150402)
XLA Ops:
  0.0 80.4 %layer.1 = bf16[384,384]{1,0:T(8,128)(2,1)S(1)} custom-call(bf16[256,128]{1,0:T(8,128)(2,1)} %tok.1, f32[48,128]{1,0:T(8,128)} %bitcast.3, bf16[48,128,384]{2,1,0:T(8,128)(2,1)} %bitcast.2, f32[1,128]{1,0:T(1,128)} %q_gain_in.1, f32[1,128]{1,0:T(1,128)} %k_gain_in.1, bf16[256,128]{1,0:T(8,128)(2,1)} %d_attn_in.1), custom_call_target="tpu_custom_call" | custom-call | flops 2600000000 | bytes 10000000 | tf_op jit(solution)/shard_map/layer/pallas_call | solution.py:486
  80.4 0.7 copy.8
